TPU v7x, 256 devices: a whole 4x4x8 slice. The times are simulated.
256 devices in a mesh: ctx: 16 (over y_hi, z), dp: 16 (over y_lo, x, core).
Axes of the slice: x: 4, y: 4 (y_hi: 2, y_lo: 2; y = y_hi * 2 + y_lo), z: 8, core: 2. Of those that a mesh axis runs over, the one named last changes fastest.
Arguments:
- inputs: bfloat16 [16, 3072, 8192], P('dp', 'ctx'), may hold values from -6 to 6
- query_saved: bfloat16 [16, 3072, 4096], P('dp', 'ctx'), may hold values from -17 to 17
- key_saved: bfloat16 [16, 3072, 512], P('dp', 'ctx'), may hold values from -17 to 17
- value_saved: bfloat16 [16, 3072, 512], P('dp', 'ctx'), may hold values from -6 to 6
- grad_out: bfloat16 [16, 3072, 4096], P('dp', 'ctx'), may hold values from -6 to 6
- value_weight: bfloat16 [8192, 512], P('dp'), may hold values from -6 to 6
- query_down_weight: bfloat16 [16, 8192], replicated, may hold values from -1.5 to 1.5
- up_q: bfloat16 [16, 4096], replicated, may hold values from -4 to 4
- value_down_weight: bfloat16 [16, 8192], replicated, may hold values from -1.5 to 1.5
- up_v: bfloat16 [16, 512], replicated, may hold values from -0.25 to 0.25
Outputs:
- grad_down_q: float32 [16, 8192], P(None, 'dp')
- grad_up_q: float32 [16, 4096], P(None, 'dp')
- grad_down_v: float32 [16, 8192], P(None, 'dp')
- grad_up_v: float32 [16, 512], P(None, 'dp')
- input_gradient: bfloat16 [16, 3072, 8192], P('dp', 'ctx')
All inputs are finite; a program needn't handle non-finite values.
Results may differ from a plain program's by a relative error of at most 0.012.
Values may be sent and summed in bfloat16 or wider, within the bound.
A program may use at most 128 MiB of HBM per device.

v0:
```python
import math

import jax
import jax.numpy as jnp
from jax import lax
from jax.sharding import PartitionSpec as P

HEAD_WIDTH = 128


adapter_scale = 2.0


def shifted(block, axis, distance):
    devices = range(lax.axis_size(axis))
    route = [((i - distance) % len(devices), i) for i in devices]
    return lax.ppermute(block, axis, route)


def group_backward(query_half, gout_half, key_window, value_window, query_base):
    row_count = query_half.shape[0]
    window_len = key_window.shape[0]
    kv_heads = key_window.shape[1]
    depth_size = key_window.shape[2]
    head_group_ratio = query_half.shape[1] // (kv_heads * depth_size)
    query_rows = query_half.reshape(row_count, kv_heads, head_group_ratio, depth_size)
    gout_rows = gout_half.reshape(row_count, kv_heads, head_group_ratio, depth_size)
    score_scale = 1.0 / math.sqrt(depth_size)
    scores = (
        jnp.einsum("tkgd,skd->kgts", query_rows, key_window, preferred_element_type=jnp.float32)
        * score_scale
    )
    query_pos = query_base + jnp.arange(row_count)
    allowed = jnp.arange(window_len)[None, :] <= query_pos[:, None]
    scores = jnp.where(allowed, scores, -jnp.inf)
    row_max = jnp.max(scores, axis=-1, keepdims=True)
    weights = jnp.exp(scores - row_max)
    probs = weights / jnp.sum(weights, axis=-1, keepdims=True)
    probs_b = probs.astype(jnp.bfloat16)
    attn_out = jnp.einsum(
        "kgts,skd->tkgd", probs_b, value_window, preferred_element_type=jnp.float32
    )
    delta = jnp.sum(gout_rows.astype(jnp.float32) * attn_out, axis=-1)
    dprob = jnp.einsum(
        "tkgd,skd->kgts", gout_rows, value_window, preferred_element_type=jnp.float32
    )
    dscore = (probs * (dprob - jnp.transpose(delta, (1, 2, 0))[..., None])).astype(jnp.bfloat16)
    dquery = (
        jnp.einsum("kgts,skd->tkgd", dscore, key_window, preferred_element_type=jnp.float32)
        * score_scale
    )
    dvalue = jnp.einsum("kgts,tkgd->skd", probs_b, gout_rows, preferred_element_type=jnp.float32)
    return (dquery.reshape(row_count, -1), dvalue.reshape(window_len, -1))


def on_device(
    inputs,
    query_saved,
    key_saved,
    value_saved,
    grad_out,
    value_weight,
    query_down_weight,
    up_q,
    value_down_weight,
    up_v,
):
    token_count = query_saved.shape[1]
    width_q = query_saved.shape[2]
    width_kv = key_saved.shape[2]
    half_q = width_q // 2
    half_kv = width_kv // 2
    half_head_count = half_kv // HEAD_WIDTH
    ctx_index = lax.axis_index("ctx")
    kv_local = jnp.stack([key_saved[0], value_saved[0]], 0)
    first_pieces = []
    second_pieces = []
    for offset in range(-3, 4):
        if offset == 0:
            first_pieces.append(kv_local[..., :half_kv])
            second_pieces.append(kv_local[..., half_kv:])
        else:
            whole_piece = shifted(kv_local, "ctx", -offset)
            first_pieces.append(whole_piece[..., :half_kv])
            second_pieces.append(whole_piece[..., half_kv:])
    half_stacks = [jnp.stack(first_pieces, 0), jnp.stack(second_pieces, 0)]
    dquery_parts = []
    padded_parts = []
    for half_index in range(2):
        group_lag = (ctx_index - 2 * half_index) % 4
        window = lax.dynamic_slice_in_dim(half_stacks[half_index], 3 - group_lag, 4, 0)
        key_window = window[:, 0].reshape(4 * token_count, half_head_count, HEAD_WIDTH)
        value_window = window[:, 1].reshape(4 * token_count, half_head_count, HEAD_WIDTH)
        qcols = slice(half_index * half_q, (half_index + 1) * half_q)
        dquery, dvalue = group_backward(
            query_saved[0][:, qcols],
            grad_out[0][:, qcols],
            key_window,
            value_window,
            group_lag * token_count,
        )
        dquery_parts.append(dquery)
        padded = jnp.zeros((7, token_count, half_kv), jnp.float32)
        padded = lax.dynamic_update_slice_in_dim(
            padded, dvalue.reshape(4, token_count, half_kv), 3 - group_lag, 0
        )
        padded_parts.append(padded)
    send_back = jnp.concatenate(padded_parts, axis=-1)
    dvalue_sum = send_back[3]
    for offset in (-3, -2, -1, 1, 2, 3):
        dvalue_sum = dvalue_sum + shifted(send_back[offset + 3], "ctx", offset)
    grad_query = jnp.concatenate(dquery_parts, axis=-1).astype(jnp.bfloat16)
    grad_value = dvalue_sum.astype(jnp.bfloat16)
    local_inputs = inputs[0]
    query_adapter_code = jnp.einsum(
        "tq,rq->tr", grad_query, up_q, preferred_element_type=jnp.float32
    ).astype(jnp.bfloat16)
    value_adapter_code = jnp.einsum(
        "tk,rk->tr", grad_value, up_v, preferred_element_type=jnp.float32
    ).astype(jnp.bfloat16)
    hidden_q = jnp.einsum(
        "td,rd->tr", local_inputs, query_down_weight, preferred_element_type=jnp.float32
    ).astype(jnp.bfloat16)
    hidden_v = jnp.einsum(
        "td,rd->tr", local_inputs, value_down_weight, preferred_element_type=jnp.float32
    ).astype(jnp.bfloat16)
    gradient_scale = adapter_scale / math.sqrt(
        lax.axis_size("dp") * lax.axis_size("ctx") * token_count
    )
    terms = (
        gradient_scale
        * jnp.einsum(
            "tr,td->rd", query_adapter_code, local_inputs, preferred_element_type=jnp.float32
        ),
        gradient_scale
        * jnp.einsum("tr,tq->rq", hidden_q, grad_query, preferred_element_type=jnp.float32),
        gradient_scale
        * jnp.einsum(
            "tr,td->rd", value_adapter_code, local_inputs, preferred_element_type=jnp.float32
        ),
        gradient_scale
        * jnp.einsum("tr,tk->rk", hidden_v, grad_value, preferred_element_type=jnp.float32),
    )
    summed = lax.psum((terms[0], terms[1], terms[2], terms[3]), "ctx")
    grad_down_q, grad_up_q, grad_down_v, grad_up_v = (
        lax.psum_scatter(summed[0], "dp", scatter_dimension=1, tiled=True),
        lax.psum_scatter(summed[1], "dp", scatter_dimension=1, tiled=True),
        lax.psum_scatter(summed[2], "dp", scatter_dimension=1, tiled=True),
        lax.psum_scatter(summed[3], "dp", scatter_dimension=1, tiled=True),
    )
    value_gradient_path = jnp.einsum(
        "tk,dk->td",
        grad_value,
        lax.all_gather(value_weight, "dp", axis=0, tiled=True),
        preferred_element_type=jnp.float32,
    )
    adapter_gradient_path = jnp.einsum(
        "tr,rd->td", query_adapter_code, query_down_weight, preferred_element_type=jnp.float32
    ) + jnp.einsum(
        "tr,rd->td", value_adapter_code, value_down_weight, preferred_element_type=jnp.float32
    )
    input_gradient = (value_gradient_path + adapter_scale * adapter_gradient_path).astype(
        jnp.bfloat16
    )[None]
    return (grad_down_q, grad_up_q, grad_down_v, grad_up_v, input_gradient)


def solution(mesh):
    in_specs = (
        P("dp", "ctx", None),
        P("dp", "ctx", None),
        P("dp", "ctx", None),
        P("dp", "ctx", None),
        P("dp", "ctx", None),
        P("dp", None),
        P(),
        P(),
        P(),
        P(),
    )
    out_specs = (P(None, "dp"), P(None, "dp"), P(None, "dp"), P(None, "dp"), P("dp", "ctx", None))
    return jax.shard_map(
        on_device, mesh=mesh, in_specs=in_specs, out_specs=out_specs, check_vma=False
    )
```

profile of v0, /device:TPU:2, one launch (start us, length us, event | category | flops | bytes accessed | tf_op | source)
XLA Modules:
  0.0 697.5 jit_solution(12091285736969077131)
XLA Ops:
  9.3 4.7 collective-permute-start
  18.6 4.6 collective-permute-start.3
  39.4 4.0 collective-permute-done
  43.5 5.0 collective-permute-start.5
  49.5 11.8 %collective-permute-done.1 = bf16[2,192,512]{2,1,0:T(8,128)(2,1)} collective-permute-done((bf16[2,192,512]{2,1,0:T(8,128)(2,1)S(1)}, bf16[2,192,512]{2,1,0:T(8,128)(2,1)}, u32[]{:S(2)}, u32[]{:S(2)}) %collective-permute-start.1) | collective-permute-done | bytes 393248 | tf_op jit(solution)/shard_map/ppermute | solution.py:17
  62.4 6.9 collective-permute-done.2
  77.7 8.5 %fusion.145 = (f32[2,8,192]{2,1,0:T(8,128)S(1)}, f32[2,8,192,768]{3,2,1,0:T(8,128)}) fusion(pred[192,768]{1,0:T(8,128)(4,1)} %iota_compare_fusion.1, bf16[192,2,8,128]{3,2,1,0:T(8,128)(2,1)} %bitcast.249, bf16[768,2,128,1]{2,1,0,3:T(2,128)(2,1)} %bitcast.252), kind=kOutput, calls=%fused_computation.170 | convolution fusion | flops 613417728 | bytes 10776576 | tf_op jit(solution)/shard_map/sub | solution.py:37
  86.1 4.4 fusion.31
  98.3 7.8 %fusion.49 = bf16[192,2,8,128]{3,0,2,1:T(8,128)(2,1)} fusion(f32[2,8,192]{2,1,0:T(8,128)S(1)} %copy.51, f32[2,8,192,768]{3,2,1,0:T(8,128)} %get-tuple-element.38, f32[2,8,192]{2,1,0:T(8,128)} %copy-done.12, bf16[192,2,8,128]{3,2,1,0:T(8,128)(2,1)} %bitcast.240, bf16[768,2,128,1]{2,1,0,3:T(2,128)(2,1)} %bitcast.254, bf16[768,2,128,1]{2,1,0,3:T(2,128)(2,1)} %bitcast.253), kind=kOutput, calls=%fused_computation.68 | convolution fusion | flops 1218183168 | bytes 11821056 | tf_op jit(solution)/shard_map/kgts,skd->tkgd/dot_general | solution.py:49
  111.3 8.5 %fusion.154 = (f32[2,8,192]{2,1,0:T(8,128)S(1)}, f32[2,8,192,768]{3,2,1,0:T(8,128)}) fusion(pred[192,768]{1,0:T(8,128)(4,1)} %iota_compare_fusion, bf16[192,2,8,128]{3,2,1,0:T(8,128)(2,1)} %bitcast.248, bf16[768,2,128,1]{2,1,0,3:T(2,128)(2,1)} %bitcast.250), kind=kOutput, calls=%fused_computation.171 | convolution fusion | flops 613417728 | bytes 10776576 | tf_op jit(solution)/shard_map/sub | solution.py:37
  119.8 4.6 fusion.32
  132.3 7.8 %fusion.52 = bf16[192,2,8,128]{3,0,2,1:T(8,128)(2,1)} fusion(f32[2,8,192]{2,1,0:T(8,128)S(1)} %copy.60, f32[2,8,192,768]{3,2,1,0:T(8,128)} %get-tuple-element.40, f32[2,8,192]{2,1,0:T(8,128)} %copy-done.13, bf16[192,2,8,128]{3,2,1,0:T(8,128)(2,1)} %bitcast.237, bf16[768,2,128,1]{2,1,0,3:T(2,128)(2,1)} %bitcast.255, bf16[768,2,128,1]{2,1,0,3:T(2,128)(2,1)S(1)} %bitcast.251), kind=kOutput, calls=%fused_computation.69 | convolution fusion | flops 1218183168 | bytes 11821056 | tf_op jit(solution)/shard_map/kgts,skd->tkgd/dot_general | solution.py:49
  156.1 8.8 %collective-permute-start.10 = (f32[192,512]{1,0:T(8,128)S(1)}, f32[192,512]{1,0:T(8,128)S(1)}, u32[]{:S(2)}, u32[]{:S(2)}) collective-permute-start(f32[192,512]{1,0:T(8,128)S(1)} %get-tuple-element.14), channel_id=1, source_target_pairs={{224,0},{240,16},{0,32},{16,48},{32,64},{48,80},{64,96},{80,112},{... | collective-permute-start | bytes 1179656 | tf_op jit(solution)/shard_map/ppermute | solution.py:17
  164.9 5.6 collective-permute-start.8
  171.6 20.5 %collective-permute-done.11 = f32[192,512]{1,0:T(8,128)S(1)} collective-permute-done((f32[192,512]{1,0:T(8,128)S(1)}, f32[192,512]{1,0:T(8,128)S(1)}, u32[]{:S(2)}, u32[]{:S(2)}) %collective-permute-start.11) | collective-permute-done | bytes 393248 | tf_op jit(solution)/shard_map/ppermute | solution.py:17
  193.1 10.7 %collective-permute-done.10 = f32[192,512]{1,0:T(8,128)S(1)} collective-permute-done((f32[192,512]{1,0:T(8,128)S(1)}, f32[192,512]{1,0:T(8,128)S(1)}, u32[]{:S(2)}, u32[]{:S(2)}) %collective-permute-start.10) | collective-permute-done | bytes 393248 | tf_op jit(solution)/shard_map/ppermute | solution.py:17
  203.8 10.9 %collective-permute-done.9 = f32[192,512]{1,0:T(8,128)S(1)} collective-permute-done((f32[192,512]{1,0:T(8,128)S(1)}, f32[192,512]{1,0:T(8,128)S(1)}, u32[]{:S(2)}, u32[]{:S(2)}) %collective-permute-start.9) | collective-permute-done | bytes 393248 | tf_op jit(solution)/shard_map/ppermute | solution.py:17
  237.0 45.6 %reduce-scatter.13.cloned.1.call-done = f32[32,16]{1,0:T(8,128)} async-done(((f32[512,16]{1,0:T(8,128)}), f32[32,16]{1,0:T(8,128)}) %reduce-scatter.13.cloned.1.call-update) | async-done | bytes 2064
  284.0 62.4 %reduce-scatter.9.cloned.1.call-done = f32[16,256]{1,0:T(8,128)} async-done(((f32[16,4096]{1,0:T(8,128)}), f32[16,256]{1,0:T(8,128)}) %reduce-scatter.9.cloned.1.call-update) | async-done | bytes 16400 | tf_op jit(solution)/shard_map/reduce_scatter | solution.py:147
  346.4 64.8 %reduce-scatter.7.cloned.1.call-done = f32[16,512]{1,0:T(8,128)} async-done(((f32[16,8192]{1,0:T(8,128)}), f32[16,512]{1,0:T(8,128)}) %reduce-scatter.7.cloned.1.call-update) | async-done | bytes 32784 | tf_op jit(solution)/shard_map/reduce_scatter | solution.py:146
  411.2 64.2 %reduce-scatter.11.cloned.1.call-done = f32[16,512]{1,0:T(8,128)} async-done(((f32[16,8192]{1,0:T(8,128)}), f32[16,512]{1,0:T(8,128)}) %reduce-scatter.11.cloned.1.call-update) | async-done | bytes 32784 | tf_op jit(solution)/shard_map/reduce_scatter | solution.py:148
  475.4 58.7 %all-gather.2.cloned.1.call-done = bf16[8192,512]{1,0:T(8,128)(2,1)} async-done(((bf16[512,512]{1,0:T(8,128)(2,1)}), bf16[8192,512]{1,0:T(8,128)(2,1)}) %all-gather.2.cloned.1.call-update) | async-done | bytes 8388624 | tf_op jit(solution)/shard_map/all_gather | solution.py:154
  534.1 9.7 %fusion.4 = bf16[1,192,8192]{2,1,0:T(8,128)(2,1)} fusion(f32[192,8192]{1,0:T(8,128)} %fusion.2, bf16[192,512]{1,0:T(8,128)(2,1)S(1)} %fusion.116, bf16[8192,512]{1,0:T(8,128)(2,1)} %all-gather.2.cloned.1.call-done), kind=kOutput, calls=%fused_computation.6 | convolution fusion | flops 1613758464 | bytes 18022400 | tf_op jit(solution)/shard_map/tk,dk->td/dot_general | solution.py:151
  543.8 141.3 %all-reduce.3.cloned.1.call-done = (f32[16,512]{1,0:T(8,128)}, f32[16,256]{1,0:T(8,128)}, f32[16,512]{1,0:T(8,128)}, f32[16,32]{1,0:T(8,128)}) async-done(((f32[16,512]{1,0:T(8,128)}, f32[16,256]{1,0:T(8,128)}, f32[16,512]{1,0:T(8,128)}, f32[16,32]{1,0:T(8,128)}), (f32[16,512]{1,0:T(8,128)}, f32[16,256]{1,0:T(8,128)}, f32[16,512]{1,0:T(8,128)}, f32[16,32]{1,0:T(8,128)})) %all-reduce.3.cloned.1.call-update) | async-done | bytes 83984 | tf_op jit(solution)/shard_map/psum | solution.py:144
  (111 shorter events, 101.2 us)
Async XLA Ops:
  7.2 211.6 %copy-start = (bf16[1,192,8192]{2,1,0:T(8,128)(2,1)S(1)}, bf16[1,192,8192]{2,1,0:T(8,128)(2,1)}, u32[]{:S(2)}) copy-start(bf16[1,192,8192]{2,1,0:T(8,128)(2,1)} %param.10) | copy-start | bytes 9437188
  7.2 275.4 %reduce-scatter.13.cloned.1.call-start = ((), (), s32[]{:S(2)}) async-start(), calls=%async_computation.8 | async-start | bytes 278528
  9.3 34.2 %collective-permute-start = (bf16[2,192,512]{2,1,0:T(8,128)(2,1)S(1)}, bf16[2,192,512]{2,1,0:T(8,128)(2,1)}, u32[]{:S(2)}, u32[]{:S(2)}) collective-permute-start(bf16[2,192,512]{2,1,0:T(8,128)(2,1)S(1)} %constant_dynamic-update-slice_fusion), channel_id=1, source_target_pairs={{208,0},{224,16},{240,32},{0,48},{16,64},{32,80},{48,96},{64,112},... | collective-permute-start | bytes 1179656 | tf_op jit(solution)/shard_map/ppermute | solution.py:17
  14.0 47.4 %collective-permute-start.1 = (bf16[2,192,512]{2,1,0:T(8,128)(2,1)S(1)}, bf16[2,192,512]{2,1,0:T(8,128)(2,1)}, u32[]{:S(2)}, u32[]{:S(2)}) collective-permute-start(bf16[2,192,512]{2,1,0:T(8,128)(2,1)S(1)} %constant_dynamic-update-slice_fusion), channel_id=1, source_target_pairs={{224,0},{240,16},{0,32},{16,48},{32,64},{48,80},{64,96},{80,112},{... | collective-permute-start | bytes 1179656 | tf_op jit(solution)/shard_map/ppermute | solution.py:17
  17.6 51.8 %collective-permute-start.2 = (bf16[2,192,512]{2,1,0:T(8,128)(2,1)S(1)}, bf16[2,192,512]{2,1,0:T(8,128)(2,1)}, u32[]{:S(2)}, u32[]{:S(2)}) collective-permute-start(bf16[2,192,512]{2,1,0:T(8,128)(2,1)S(1)} %constant_dynamic-update-slice_fusion), channel_id=1, source_target_pairs={{240,0},{0,16},{16,32},{32,48},{48,64},{64,80},{80,96},{96,112},{1... | collective-permute-start | bytes 1179656 | tf_op jit(solution)/shard_map/ppermute | solution.py:17
  18.6 51.8 %collective-permute-start.3 = (bf16[2,192,512]{2,1,0:T(8,128)(2,1)S(1)}, bf16[2,192,512]{2,1,0:T(8,128)(2,1)}, u32[]{:S(2)}, u32[]{:S(2)}) collective-permute-start(bf16[2,192,512]{2,1,0:T(8,128)(2,1)S(1)} %constant_dynamic-update-slice_fusion), channel_id=1, source_target_pairs={{16,0},{32,16},{48,32},{64,48},{80,64},{96,80},{112,96},{128,112},... | collective-permute-start | bytes 1179656 | tf_op jit(solution)/shard_map/ppermute | solution.py:17
  23.2 48.3 %collective-permute-start.4 = (bf16[2,192,512]{2,1,0:T(8,128)(2,1)S(1)}, bf16[2,192,512]{2,1,0:T(8,128)(2,1)}, u32[]{:S(2)}, u32[]{:S(2)}) collective-permute-start(bf16[2,192,512]{2,1,0:T(8,128)(2,1)S(1)} %constant_dynamic-update-slice_fusion), channel_id=1, source_target_pairs={{32,0},{48,16},{64,32},{80,48},{96,64},{112,80},{128,96},{144,112}... | collective-permute-start | bytes 1179656 | tf_op jit(solution)/shard_map/ppermute | solution.py:17
  43.5 29.4 %collective-permute-start.5 = (bf16[2,192,512]{2,1,0:T(8,128)(2,1)S(1)}, bf16[2,192,512]{2,1,0:T(8,128)(2,1)S(1)}, u32[]{:S(2)}, u32[]{:S(2)}) collective-permute-start(bf16[2,192,512]{2,1,0:T(8,128)(2,1)S(1)} %constant_dynamic-update-slice_fusion), channel_id=1, source_target_pairs={{48,0},{64,16},{80,32},{96,48},{112,64},{128,80},{144,96},{160,112... | collective-permute-start | bytes 1179656 | tf_op jit(solution)/shard_map/ppermute | solution.py:17
  119.8 4.6 copy-start.13
  119.8 4.6 copy-start.1
  127.4 4.8 copy-start.7
  154.7 15.8 %copy-start.3 = (bf16[192,2,8,128]{3,2,1,0:T(8,128)(2,1)S(1)}, bf16[192,2,8,128]{3,2,1,0:T(8,128)(2,1)}, u32[]{:S(2)}) copy-start(bf16[192,2,8,128]{3,2,1,0:T(8,128)(2,1)} %copy.53) | copy-start | bytes 2359300
  154.8 37.3 %copy-start.4 = (bf16[192,2,8,128]{3,2,1,0:T(8,128)(2,1)S(1)}, bf16[192,2,8,128]{3,2,1,0:T(8,128)(2,1)}, u32[]{:S(2)}) copy-start(bf16[192,2,8,128]{3,2,1,0:T(8,128)(2,1)} %copy.62) | copy-start | bytes 2359300
  155.1 37.0 %collective-permute-start.11 = (f32[192,512]{1,0:T(8,128)S(1)}, f32[192,512]{1,0:T(8,128)S(1)}, u32[]{:S(2)}, u32[]{:S(2)}) collective-permute-start(f32[192,512]{1,0:T(8,128)S(1)} %get-tuple-element.13), channel_id=1, source_target_pairs={{208,0},{224,16},{240,32},{0,48},{16,64},{32,80},{48,96},{64,112},... | collective-permute-start | bytes 1179656 | tf_op jit(solution)/shard_map/ppermute | solution.py:17
  156.1 47.7 %collective-permute-start.10 = (f32[192,512]{1,0:T(8,128)S(1)}, f32[192,512]{1,0:T(8,128)S(1)}, u32[]{:S(2)}, u32[]{:S(2)}) collective-permute-start(f32[192,512]{1,0:T(8,128)S(1)} %get-tuple-element.14), channel_id=1, source_target_pairs={{224,0},{240,16},{0,32},{16,48},{32,64},{48,80},{64,96},{80,112},{... | collective-permute-start | bytes 1179656 | tf_op jit(solution)/shard_map/ppermute | solution.py:17
  164.9 49.8 %collective-permute-start.9 = (f32[192,512]{1,0:T(8,128)S(1)}, f32[192,512]{1,0:T(8,128)S(1)}, u32[]{:S(2)}, u32[]{:S(2)}) collective-permute-start(f32[192,512]{1,0:T(8,128)S(1)} %get-tuple-element.12), channel_id=1, source_target_pairs={{240,0},{0,16},{16,32},{32,48},{48,64},{64,80},{80,96},{96,112},{1... | collective-permute-start | bytes 1179656 | tf_op jit(solution)/shard_map/ppermute | solution.py:17
  164.9 49.8 %collective-permute-start.8 = (f32[192,512]{1,0:T(8,128)S(1)}, f32[192,512]{1,0:T(8,128)S(1)}, u32[]{:S(2)}, u32[]{:S(2)}) collective-permute-start(f32[192,512]{1,0:T(8,128)S(1)} %get-tuple-element.11), channel_id=1, source_target_pairs={{16,0},{32,16},{48,32},{64,48},{80,64},{96,80},{112,96},{128,112},... | collective-permute-start | bytes 1179656 | tf_op jit(solution)/shard_map/ppermute | solution.py:17
  170.5 44.2 %collective-permute-start.7 = (f32[192,512]{1,0:T(8,128)S(1)}, f32[192,512]{1,0:T(8,128)S(1)}, u32[]{:S(2)}, u32[]{:S(2)}) collective-permute-start(f32[192,512]{1,0:T(8,128)S(1)} %get-tuple-element.10), channel_id=1, source_target_pairs={{32,0},{48,16},{64,32},{80,48},{96,64},{112,80},{128,96},{144,112}... | collective-permute-start | bytes 1179656 | tf_op jit(solution)/shard_map/ppermute | solution.py:17
  192.0 26.5 %collective-permute-start.6 = (f32[192,512]{1,0:T(8,128)S(1)}, f32[192,512]{1,0:T(8,128)S(1)}, u32[]{:S(2)}, u32[]{:S(2)}) collective-permute-start(f32[192,512]{1,0:T(8,128)S(1)} %get-tuple-element.9), channel_id=1, source_target_pairs={{48,0},{64,16},{80,32},{96,48},{112,64},{128,80},{144,96},{160,112... | collective-permute-start | bytes 1179656 | tf_op jit(solution)/shard_map/ppermute | solution.py:17
  221.8 124.6 %reduce-scatter.9.cloned.1.call-start = ((), (), s32[]{:S(2)}) async-start(), calls=%async_computation.6 | async-start | bytes 278528 | tf_op jit(solution)/shard_map/reduce_scatter | solution.py:147
  225.7 185.4 %reduce-scatter.7.cloned.1.call-start = ((), (), s32[]{:S(2)}) async-start(), calls=%async_computation.5 | async-start | bytes 557056 | tf_op jit(solution)/shard_map/reduce_scatter | solution.py:146
  229.1 246.3 %reduce-scatter.11.cloned.1.call-start = ((), (), s32[]{:S(2)}) async-start(), calls=%async_computation.7 | async-start | bytes 557056 | tf_op jit(solution)/shard_map/reduce_scatter | solution.py:148
  230.6 303.5 %all-gather.2.cloned.1.call-start = ((), (), s32[]{:S(2)}) async-start(), calls=%async_computation.4 | async-start | bytes 8912896 | tf_op jit(solution)/shard_map/all_gather | solution.py:154
  231.2 453.9 %all-reduce.3.cloned.1.call-start = ((), (), s32[]{:S(2)}) async-start(), calls=%async_computation.9 | async-start | bytes 180224 | tf_op jit(solution)/shard_map/psum | solution.py:144
  (8 other events, 25.7 us)
Sparse Core Ops, SparseCore 0:
  221.9 60.6 reduce-scatter.12
  285.2 61.0 reduce-scatter.8
  349.5 61.6 reduce-scatter.6
  413.7 61.6 reduce-scatter.10
  477.1 57.0 all-gather.1
  537.4 147.6 all-reduce.2
where the time goes:
time: 706 us; the launch traced here: 698 us
  waiting for transfers between devices  507 us (72%)
  matrix products  72.1 us (10%)
  local copies, waits for them, and re-layouts  57.9 us (8%)
  starting transfers between devices  35.1 us (5%)
  between operations  14.6 us (2%)
  other arithmetic  11.3 us (2%)
    psum x1, waiting for transfers between devices, on_device(): summed = lax.psum((terms[0], terms[1], terms[2], terms[3]), 'ctx')  141 us
    ppermute x12, waiting for transfers between devices, shifted(): return lax.ppermute(block, axis, route)  69 us
    reduce_scatter x1, waiting for transfers between devices, on_device(): lax.psum_scatter(summed[0], 'dp', scatter_dimension=1, tiled=True)  64.8 us
    reduce_scatter x1, waiting for transfers between devices, on_device(): lax.psum_scatter(summed[2], 'dp', scatter_dimension=1, tiled=True)  64.2 us
    reduce_scatter x1, waiting for transfers between devices, on_device(): lax.psum_scatter(summed[1], 'dp', scatter_dimension=1, tiled=True)  62.4 us
    all_gather x1, waiting for transfers between devices, on_device(): lax.all_gather(value_weight, 'dp', axis=0, tiled=True)  58.7 us
    unnamed x7, waiting for transfers between devices  46.2 us
    ppermute x12, starting transfers between devices, shifted(): return lax.ppermute(block, axis, route)  34.8 us
  transfers between devices with their start and end apart: 18, of which 14 were waited for; matrix products, arithmetic and copies ran while one was open for 7% of the time, Pallas kernels for 0%

commit v1 on v0

v1 whole, which is shorter than its diff:
```python
import functools
import math

import jax
import jax.numpy as jnp
from jax import lax
from jax.experimental import pallas as pl
from jax.experimental.pallas import tpu as pltpu
from jax.sharding import PartitionSpec as P

MESH = pl.DeviceIdType.MESH
F32 = jnp.float32
BF16 = jnp.bfloat16

CTX = 16
DP = 16
T = 192
D = 128
LANES = 4 * T
QUADS = 8
WIDTH = 8192
SHARD = WIDTH // DP
DQ = 4096
DKV = 512
ADAPTER_SCALE = 2.0
CHUNK = 32


def nt(a, b):
    return lax.dot_general(a, b, (((1,), (1,)), ((), ())), preferred_element_type=F32)


def nn(a, b):
    return jnp.dot(a, b, preferred_element_type=F32)


def kernel(
    x_hbm,
    q_hbm,
    k_hbm,
    v_hbm,
    g_hbm,
    w_hbm,
    qdw_hbm,
    upq_hbm,
    vdw_hbm,
    upv_hbm,
    down_q_out,
    up_q_out,
    down_v_out,
    up_v_out,
    dx_hbm,
    x,
    q,
    g,
    kvw,
    w,
    dw,
    upq,
    upv,
    bias,
    s_buf,
    dp_buf,
    pb_buf,
    ds_buf,
    kt,
    dv_acc,
    dv_own,
    dv_snd,
    dv_rcv,
    gq,
    gv,
    hid,
    ht4,
    codes,
    term_q,
    term_v,
    rcv_q,
    rcv_v,
    rs_src,
    rs_rcv,
    ag,
    dx,
    loc_sem,
    kv_ssem,
    kv_rsem,
    w_ssem,
    w_rsem,
    dv_ssem,
    dv_rsem,
    t_ssem,
    t_rsem,
    r_ssem,
    r_rsem,
    out_sem,
):
    c = lax.axis_index("ctx")
    p = lax.axis_index("dp")
    right = lax.rem(c + 1, CTX)
    scale = 1.0 / math.sqrt(D)
    exp2_scale = scale * math.log2(math.e)

    def remote(src, dst, ssem, rsem, ctx, dp):
        return pltpu.make_async_remote_copy(
            src_ref=src,
            dst_ref=dst,
            send_sem=ssem,
            recv_sem=rsem,
            device_id=(ctx, dp),
            device_id_type=MESH,
        )

    loads = []

    def load(src, dst):
        copy = pltpu.make_async_copy(src, dst, loc_sem.at[len(loads)])
        copy.start()
        loads.append(copy)
        return copy

    kv_loads = []
    for half in range(2):
        for which, ref in ((0, k_hbm), (1, v_hbm)):
            for head in range(2):
                col = (half * 2 + head) * D
                kv_loads.append(load(ref.at[:, col : col + D], kvw.at[half, 0, which, head]))
    dw_loads = [load(qdw_hbm, dw.at[0:16]), load(vdw_hbm, dw.at[16:32])]
    x_load = load(x_hbm, x)
    q_load = load(q_hbm, q)
    g_load = load(g_hbm, g)
    up_loads = [load(upq_hbm, upq), load(upv_hbm, upv)]
    w_load = load(w_hbm, w.at[p])

    with jax.named_scope("greet"):
        barrier = pltpu.get_barrier_semaphore()

        def greet(off, carry):
            pl.semaphore_signal(
                barrier, inc=1, device_id=(lax.rem(c + off, CTX), p), device_id_type=MESH
            )
            pl.semaphore_signal(
                barrier, inc=1, device_id=(c, lax.rem(p + off, DP)), device_id_type=MESH
            )
            return carry

        lax.fori_loop(1, 16, greet, 0)
        pl.semaphore_wait(barrier, 30)

    lags = (lax.rem(c, 4), lax.rem(c + 2, 4))
    parity = lax.rem(c, 2)
    first_half = lax.rem(c, 4) // 2
    second_half = 1 - first_half

    def kv_copy(half, slot):
        return remote(
            kvw.at[half, slot],
            kvw.at[half, slot + 1],
            kv_ssem.at[half, slot],
            kv_rsem.at[half, slot + 1],
            right,
            p,
        )

    def kv_arrived(half, slot):
        remote(
            kvw.at[half, slot],
            kvw.at[half, slot],
            kv_ssem.at[half, slot],
            kv_rsem.at[half, slot],
            right,
            p,
        ).wait_recv()

    with jax.named_scope("kv_send"):
        for copy in kv_loads:
            copy.wait()
        for half in range(2):

            @pl.when(lags[half] < 3)
            def _(half=half):
                kv_copy(half, 0).start()

    core = lax.rem(p, 2)
    px = lax.rem(p // 2, 4)
    py = p // 8

    def at(dy, dx_, dc):
        yy = lax.rem(py + dy, 2)
        xx = lax.rem(px + dx_ + 4, 4)
        cc = lax.rem(core + dc, 2)
        return yy * 8 + xx * 2 + cc

    x_up, x_dn, y_nb, sib = at(0, 1, 0), at(0, -1, 0), at(1, 0, 0), at(0, 0, 1)
    origin = [at(0, -1, 0), at(0, 1, 0), at(1, 0, 0), at(0, 2, 0), at(1, -1, 0), at(1, 1, 0), at(1, 2, 0)]
    origin = origin + [at(0, 0, 1)] + [
        at(0, -1, 1),
        at(0, 1, 1),
        at(1, 0, 1),
        at(0, 2, 1),
        at(1, -1, 1),
        at(1, 1, 1),
        at(1, 2, 1),
    ]

    def w_copy(kind, shard, target, src=None):
        block = w.at[shard]
        return remote(
            block if src is None else src, block, w_ssem.at[kind], w_rsem.at[kind], c, target
        )

    def w_arrived(kind):
        remote(
            w.at[origin[kind]], w.at[origin[kind]], w_ssem.at[kind], w_rsem.at[kind], c, sib
        ).wait_recv()

    w_sends = {
        0: w_copy(0, p, x_up, w_hbm),
        1: w_copy(1, p, x_dn, w_hbm),
        2: w_copy(2, p, y_nb, w_hbm),
        7: w_copy(7, p, sib, w_hbm),
        3: w_copy(3, origin[1], x_dn),
        4: w_copy(4, origin[2], x_up),
        5: w_copy(5, origin[1], y_nb),
        6: w_copy(6, origin[3], y_nb),
    }
    for i in range(7):
        w_sends[8 + i] = w_copy(8 + i, origin[i], sib)
    for kind in (0, 1, 2, 7):
        w_sends[kind].start()

    with jax.named_scope("bias"):
        row = lax.broadcasted_iota(jnp.int32, (T, LANES), 0)
        lane = lax.broadcasted_iota(jnp.int32, (T, LANES), 1)
        turn = (
            (lane >= T).astype(jnp.int32)
            + (lane >= 2 * T).astype(jnp.int32)
            + (lane >= 3 * T).astype(jnp.int32)
        )
        bias[...] = jnp.where(row <= lane - turn * T, 0.0, -jnp.inf).astype(F32)

    with jax.named_scope("hidden"):
        for copy in dw_loads:
            copy.wait()
        x_load.wait()

        def hidden_step(i, acc):
            cols = pl.ds(pl.multiple_of(i * 1024, 1024), 1024)
            return acc + nt(dw[:, cols], x[:, cols])

        hidden = lax.fori_loop(0, 8, hidden_step, jnp.zeros((32, T), F32))
        hid[...] = jnp.zeros_like(hid)
        hid[:, 0:T] = hidden.astype(BF16).astype(F32)
        ht4[...] = jnp.zeros_like(ht4)
        padded = hid[0:16, :]
        turned = pltpu.roll(padded, 64, 1)
        ht4[0:16, 0:256] = padded.astype(BF16)
        ht4[16:32, 128:384] = turned.astype(BF16)
        ht4[32:48, 384:640] = padded.astype(BF16)
        ht4[48:64, 512:768] = turned.astype(BF16)

    with jax.named_scope("kv_forward_1"):
        for half in range(2):

            @pl.when(lags[half] >= 1)
            def _(half=half):
                kv_arrived(half, 1)

            @pl.when((lags[half] >= 1) & (lags[half] <= 2))
            def _(half=half):
                kv_copy(half, 1).start()

        q_load.wait()
        g_load.wait()

    def four_heads(ref, quad):
        block = ref[:, pl.ds(pl.multiple_of(quad * 512, 512), 512)]
        return jnp.concatenate([block[:, i * D : (i + 1) * D] for i in range(4)], axis=0)

    def attend(half, kv, nk):
        n = nk * T

        keys = kvw[half, 0:nk, 0, kv].reshape(n, D)
        kt[:, 0:n] = keys.T
        dv_acc[0:n] = jnp.zeros((n, D), F32)

        def quad_step(i, carry):
            quad = half * 4 + kv * 2 + i
            q4 = four_heads(q, quad)
            top = None
            for d in range(nk):
                s = nt(kvw[half, d, 0, kv], q4)
                if d == 0:
                    s = s + bias[...]
                s_buf[d * T : (d + 1) * T] = s
                m = jnp.max(s, axis=0, keepdims=True)
                top = m if top is None else jnp.maximum(top, m)
            g4 = four_heads(g, quad)
            for d in range(nk):
                dp_buf[d * T : (d + 1) * T] = nt(kvw[half, d, 1, kv], g4)

            def exp_step(j, sums):
                rows = pl.ds(pl.multiple_of(j * CHUNK, CHUNK), CHUNK)
                e = jnp.exp2((s_buf[rows] - top) * exp2_scale)
                s_buf[rows] = e
                return (
                    sums[0] + jnp.sum(e.reshape(CHUNK // 8, 8, LANES), axis=0),
                    sums[1] + jnp.sum((e * dp_buf[rows]).reshape(CHUNK // 8, 8, LANES), axis=0),
                )

            zero = jnp.zeros((8, LANES), F32)
            total, weighted = lax.fori_loop(0, n // CHUNK, exp_step, (zero, zero), unroll=True)
            inv = 1.0 / jnp.sum(total, axis=0, keepdims=True)
            delta = jnp.sum(weighted, axis=0, keepdims=True) * inv

            def grad_step(j, carry):
                rows = pl.ds(pl.multiple_of(j * CHUNK, CHUNK), CHUNK)
                probs = s_buf[rows] * inv
                pb_buf[rows] = probs.astype(BF16)
                ds_buf[rows] = (probs * (dp_buf[rows] - delta)).astype(BF16)
                return carry

            lax.fori_loop(0, n // CHUNK, grad_step, 0, unroll=True)
            dv_acc[0:n] += nn(pb_buf[0:n], g4)
            gq[quad] = (nn(kt[:, 0:n], ds_buf[0:n]) * scale).astype(BF16)
            return carry

        lax.fori_loop(0, 2, quad_step, 0)
        dv_own[half, kv] = dv_acc[0:T]
        for d in range(1, nk):
            dv_snd[half, d - 1, kv] = dv_acc[d * T : (d + 1) * T].astype(BF16)
            dv_copy(half, d, kv).start()

    def dv_copy(half, d, kv):
        return remote(
            dv_snd.at[half, d - 1, kv],
            dv_rcv.at[half, d - 1, kv],
            dv_ssem.at[half, d - 1, kv],
            dv_rsem.at[half, d - 1, kv],
            lax.rem(c + CTX - d, CTX),
            p,
        )

    def first_step(kv, carry):
        @pl.when(parity == 0)
        def _():
            attend(first_half, kv, 1)

        @pl.when(parity == 1)
        def _():
            attend(first_half, kv, 2)

        return carry

    with jax.named_scope("attend_first"):
        lax.fori_loop(0, 2, first_step, 0)

    with jax.named_scope("kv_forward_2"):
        kv_arrived(second_half, 2)

        @pl.when(parity == 0)
        def _():
            kv_copy(second_half, 2).start()

    with jax.named_scope("w_forward_1"):
        for kind in (0, 1, 2):
            w_arrived(kind)
        for kind in (3, 4, 5, 8, 9, 10):
            w_sends[kind].start()

    with jax.named_scope("kv_last"):
        @pl.when(parity == 1)
        def _():
            kv_arrived(second_half, 3)

    def second_step(kv, carry):
        @pl.when(parity == 0)
        def _():
            attend(second_half, kv, 3)

        @pl.when(parity == 1)
        def _():
            attend(second_half, kv, 4)

        @pl.when(kv == 0)
        def _():
            with jax.named_scope("w_forward_2"):
                for kind in (3, 4, 5):
                    w_arrived(kind)
                for kind in (6, 11, 12, 13):
                    w_sends[kind].start()

        return carry

    with jax.named_scope("attend_second"):
        lax.fori_loop(0, 2, second_step, 0)

    with jax.named_scope("query_terms"):
        for copy in up_loads:
            copy.wait()
        flat_gq = gq[...].reshape(QUADS * D, LANES)
        up4 = jnp.concatenate(
            [
                jnp.concatenate(
                    [upq[:, (4 * i + j) * D : (4 * i + j + 1) * D] for i in range(QUADS)], axis=1
                )
                for j in range(4)
            ],
            axis=0,
        )
        r = nn(up4, flat_gq)
        code_q = (
            r[0:16, 0:256]
            + pltpu.roll(r[16:32, 128:384], 192, 1)
            + r[32:48, 384:640]
            + pltpu.roll(r[48:64, 512:768], 192, 1)
        )
        codes[...] = jnp.zeros_like(codes)
        codes[0:16, :] = code_q
        code_qt = codes[0:16, 0:T].astype(BF16)
        up_terms = nt(ht4[...], flat_gq)
        for i in range(DP):
            lo = 32 * (i % 2)
            col = D * (i // 2)
            term_q[i, :, 512:640] = up_terms[lo : lo + 16, col : col + D].astype(BF16)
            term_q[i, :, 640:768] = up_terms[lo + 16 : lo + 32, col : col + D].astype(BF16)

    def down_terms(term, code):
        def step(i, carry):
            cols = pl.ds(pl.multiple_of(i * SHARD, SHARD), SHARD)
            term[i, :, 0:SHARD] = nn(code, x[:, cols]).astype(BF16)
            return carry

        lax.fori_loop(0, DP, step, 0)

    def term_copy(which, off):
        target = lax.rem(p + off, DP)
        term, rcv = ((term_q, rcv_q), (term_v, rcv_v))[which]
        return remote(
            term.at[target],
            rcv.at[off],
            t_ssem.at[which, off],
            t_rsem.at[which, off],
            c,
            target,
        )

    def each(fn):
        def step(off, carry):
            fn(off)
            return carry

        lax.fori_loop(1, 16, step, 0)

    with jax.named_scope("query_down"):
        down_terms(term_q, code_qt)
        each(lambda off: term_copy(0, off).start())
        rcv_q[0] = term_q[p]

    with jax.named_scope("w_forward_3"):
        w_arrived(6)
        w_sends[14].start()

    with jax.named_scope("value_gradient"):
        for half in range(2):
            for d in range(1, 4):

                @pl.when(lags[half] + d <= 3)
                def _(half=half, d=d):
                    for kv in range(2):
                        dv_copy(half, d, kv).wait_recv()
                        dv_own[half, kv] += dv_rcv[half, d - 1, kv].astype(F32)

            for kv in range(2):
                col = (half * 2 + kv) * D
                gv[:, col : col + D] = dv_own[half, kv].astype(BF16)

        code_vt = nt(upv[...], gv[...])
        codes[16:32, 0:T] = code_vt
        code_vt = code_vt.astype(BF16)
        hidden_v = hid[16:32, 0:T].astype(BF16)
        up_v_terms = nn(hidden_v, gv[...])
        for i in range(DP):
            col = D * (i // 4)
            term_v[i, :, 512:640] = up_v_terms[:, col : col + D].astype(BF16)
        down_terms(term_v, code_vt)
        each(lambda off: term_copy(1, off).start())
        rcv_v[0] = term_v[p]

    with jax.named_scope("w_wait"):
        w_load.wait()
        for kind in range(7, 15):
            w_arrived(kind)
        code = (ADAPTER_SCALE * codes[...].astype(BF16).astype(F32)).T
        code = code[0:T, :].astype(BF16)

    def out_copy(i):
        cols = pl.ds(pl.multiple_of(i * SHARD, SHARD), SHARD)
        return pltpu.make_async_copy(dx.at[:, cols], dx_hbm.at[:, cols], out_sem.at[i])

    def dx_step(i, carry):
        cols = pl.ds(pl.multiple_of(i * SHARD, SHARD), SHARD)
        dx[:, cols] = (nt(gv[...], w[i]) + nn(code, dw[:, cols])).astype(BF16)
        out_copy(i).start()
        return carry

    with jax.named_scope("dx_1"):
        lax.fori_loop(0, 8, dx_step, 0)

    with jax.named_scope("sum_dp"):
        each(lambda off: term_copy(0, off).wait_recv())
        each(lambda off: term_copy(1, off).wait_recv())
        rs_src[...] = jnp.zeros_like(rs_src)
        sum_q = jnp.sum(rcv_q[...].astype(F32), axis=0)
        sum_v = jnp.sum(rcv_v[...].astype(F32), axis=0)
        for j in range(6):
            rs_src[:, j, :] = sum_q[:, j * D : (j + 1) * D]
        for j in range(5):
            rs_src[:, 6 + j, :] = sum_v[:, j * D : (j + 1) * D]

    def row_copy(off):
        target = lax.rem(c + off, CTX)
        return remote(
            rs_src.at[target], rs_rcv.at[off], r_ssem.at[0, off], r_rsem.at[0, off], target, p
        )

    def sum_copy(off, src=None):
        target = lax.rem(c + off, CTX)
        return remote(ag.at[c], ag.at[c], r_ssem.at[1, off], r_rsem.at[1, off], target, p)

    def sum_arrived(off):
        src = lax.rem(c + CTX - off, CTX)
        remote(ag.at[src], ag.at[src], r_ssem.at[1, off], r_rsem.at[1, off], src, p).wait_recv()

    each(lambda off: row_copy(off).start())
    rs_rcv[0] = rs_src[c]

    with jax.named_scope("dx_2"):
        lax.fori_loop(8, 12, dx_step, 0)

    with jax.named_scope("sum_ctx"):
        each(lambda off: row_copy(off).wait_recv())
        gradient_scale = ADAPTER_SCALE / math.sqrt(DP * CTX * T)
        ag[c] = jnp.sum(rs_rcv[...], axis=0) * gradient_scale
        each(lambda off: sum_copy(off).start())

    with jax.named_scope("dx_3"):
        lax.fori_loop(12, 16, dx_step, 0)

    with jax.named_scope("outputs"):
        each(sum_arrived)
        for j in range(4):
            down_q_out[:, j * D : (j + 1) * D] = ag[:, j, :]
            down_v_out[:, j * D : (j + 1) * D] = ag[:, 6 + j, :]
        for j in range(2):
            up_q_out[:, j * D : (j + 1) * D] = ag[:, 4 + j, :]
        piece = ag[:, 10, :]
        for j in range(4):

            @pl.when(lax.rem(p, 4) == j)
            def _(j=j):
                up_v_out[...] = piece[:, 32 * j : 32 * (j + 1)]

    with jax.named_scope("drain"):
        def out_wait(i, carry):
            out_copy(i).wait()
            return carry

        lax.fori_loop(0, DP, out_wait, 0)
        for half in range(2):

            @pl.when(lags[half] < 3)
            def _(half=half):
                kv_copy(half, 0).wait_send()

            @pl.when((lags[half] >= 1) & (lags[half] <= 2))
            def _(half=half):
                kv_copy(half, 1).wait_send()

            for d in range(1, 4):

                @pl.when(lags[half] >= d)
                def _(half=half, d=d):
                    for kv in range(2):
                        dv_copy(half, d, kv).wait_send()

        @pl.when(parity == 0)
        def _():
            kv_copy(second_half, 2).wait_send()

        for kind in range(15):
            w_sends[kind].wait_send()

        def sent(off):
            term_copy(0, off).wait_send()
            term_copy(1, off).wait_send()
            row_copy(off).wait_send()
            sum_copy(off).wait_send()

        each(sent)


def on_device(
    inputs,
    query_saved,
    key_saved,
    value_saved,
    grad_out,
    value_weight,
    query_down_weight,
    up_q,
    value_down_weight,
    up_v,
):
    out = pl.pallas_call(
        kernel,
        out_shape=(
            jax.ShapeDtypeStruct((16, SHARD), F32),
            jax.ShapeDtypeStruct((16, DQ // DP), F32),
            jax.ShapeDtypeStruct((16, SHARD), F32),
            jax.ShapeDtypeStruct((16, DKV // DP), F32),
            jax.ShapeDtypeStruct((T, WIDTH), BF16),
        ),
        in_specs=[pl.BlockSpec(memory_space=pl.ANY)] * 10,
        out_specs=[pl.BlockSpec(memory_space=pltpu.VMEM)] * 4
        + [pl.BlockSpec(memory_space=pl.ANY)],
        scratch_shapes=[
            pltpu.VMEM((T, WIDTH), BF16),
            pltpu.VMEM((T, DQ), BF16),
            pltpu.VMEM((T, DQ), BF16),
            pltpu.VMEM((2, 4, 2, 2, T, D), BF16),
            pltpu.VMEM((DP, SHARD, DKV), BF16),
            pltpu.VMEM((32, WIDTH), BF16),
            pltpu.VMEM((16, DQ), BF16),
            pltpu.VMEM((16, DKV), BF16),
            pltpu.VMEM((T, LANES), F32),
            pltpu.VMEM((4 * T, LANES), F32),
            pltpu.VMEM((4 * T, LANES), F32),
            pltpu.VMEM((4 * T, LANES), BF16),
            pltpu.VMEM((4 * T, LANES), BF16),
            pltpu.VMEM((D, 4 * T), BF16),
            pltpu.VMEM((4 * T, D), F32),
            pltpu.VMEM((2, 2, T, D), F32),
            pltpu.VMEM((2, 3, 2, T, D), BF16),
            pltpu.VMEM((2, 3, 2, T, D), BF16),
            pltpu.VMEM((QUADS, D, LANES), BF16),
            pltpu.VMEM((T, DKV), BF16),
            pltpu.VMEM((32, 256), F32),
            pltpu.VMEM((64, LANES), BF16),
            pltpu.VMEM((32, 256), F32),
            pltpu.VMEM((DP, 16, 768), BF16),
            pltpu.VMEM((DP, 16, 640), BF16),
            pltpu.VMEM((DP, 16, 768), BF16),
            pltpu.VMEM((DP, 16, 640), BF16),
            pltpu.VMEM((CTX, 16, D), F32),
            pltpu.VMEM((CTX, 16, D), F32),
            pltpu.VMEM((CTX, 16, D), F32),
            pltpu.VMEM((T, WIDTH), BF16),
            pltpu.SemaphoreType.DMA((16,)),
            pltpu.SemaphoreType.DMA((2, 4)),
            pltpu.SemaphoreType.DMA((2, 4)),
            pltpu.SemaphoreType.DMA((15,)),
            pltpu.SemaphoreType.DMA((15,)),
            pltpu.SemaphoreType.DMA((2, 3, 2)),
            pltpu.SemaphoreType.DMA((2, 3, 2)),
            pltpu.SemaphoreType.DMA((2, 16)),
            pltpu.SemaphoreType.DMA((2, 16)),
            pltpu.SemaphoreType.DMA((2, 16)),
            pltpu.SemaphoreType.DMA((2, 16)),
            pltpu.SemaphoreType.DMA((16,)),
        ],
        compiler_params=pltpu.CompilerParams(
            collective_id=0, has_side_effects=True, vmem_limit_bytes=56 * 1024 * 1024
        ),
    )(
        inputs[0],
        query_saved[0],
        key_saved[0],
        value_saved[0],
        grad_out[0],
        value_weight,
        query_down_weight,
        up_q,
        value_down_weight,
        up_v,
    )
    return out[0], out[1], out[2], out[3], out[4][None]


def solution(mesh):
    in_specs = (
        P("dp", "ctx", None),
        P("dp", "ctx", None),
        P("dp", "ctx", None),
        P("dp", "ctx", None),
        P("dp", "ctx", None),
        P("dp", None),
        P(),
        P(),
        P(),
        P(),
    )
    out_specs = (P(None, "dp"), P(None, "dp"), P(None, "dp"), P(None, "dp"), P("dp", "ctx", None))
    return jax.shard_map(
        on_device, mesh=mesh, in_specs=in_specs, out_specs=out_specs, check_vma=False
    )
```

time: 706 us -> 95.5 us (0.14)
  the two profiles are of different devices: /device:TPU:2 before, /device:TPU:1 now
where the time goes in v1:
time: 95.5 us; the launch traced here: 95.1 us
  Pallas kernels  85.3 us (89%)
  local copies, waits for them, and re-layouts  9.22 us (10%)
    pallas_call x1, Pallas kernels, on_device(): pl.pallas_call(kernel, out_shape=(jax.ShapeDtypeStruct((16, SHARD), F32),...  85.3 us
    unnamed x5, local copies, waits for them, and re-layouts  9.22 us

profile of v1, /device:TPU:1, one launch (start us, length us, event | category | flops | bytes accessed | tf_op | source)
XLA Modules:
  0.0 95.1 jit_solution(10009154625510076580)
XLA Ops:
  0.6 85.3 %shard_map.137 = (f32[16,512]{1,0:T(8,128)}, f32[16,256]{1,0:T(8,128)}, f32[16,512]{1,0:T(8,128)}, f32[16,32]{1,0:T(8,128)}, bf16[192,8192]{1,0:T(8,128)(2,1)}) custom-call(bf16[192,8192]{1,0:T(8,128)(2,1)} %bitcast.7, bf16[192,4096]{1,0:T(8,128)(2,1)} %bitcast.8, bf16[192,512]{1,0:T(8,128)(2,1)} %bitcast.10, bf16[192,512]{1,0:T(8,128)(2,1)} %bitcast.11, ...), custom_call_target="tpu_custom_call" | custom-call | tf_op jit(solution)/shard_map/pallas_call | solution.py:614
  85.9 1.4 %copy.20 = f32[16,512]{1,0:T(8,128)} copy(f32[16,512]{1,0:T(8,128)} %get-tuple-element.20) | data formatting | bytes 65536
  87.3 1.3 %copy.21 = f32[16,256]{1,0:T(8,128)} copy(f32[16,256]{1,0:T(8,128)} %get-tuple-element.21) | data formatting | bytes 32768
  88.6 1.4 %copy.22 = f32[16,512]{1,0:T(8,128)} copy(f32[16,512]{1,0:T(8,128)} %get-tuple-element.22) | data formatting | bytes 65536
  90.0 1.3 %copy.23 = f32[16,32]{1,0:T(8,128)} copy(f32[16,32]{1,0:T(8,128)} %get-tuple-element.23) | data formatting | bytes 4096
  91.3 3.9 %copy.24 = bf16[1,192,8192]{2,1,0:T(8,128)(2,1)} copy(bf16[1,192,8192]{2,1,0:T(8,128)(2,1)} %bitcast.6) | data formatting | bytes 6291456

commit v2 on v1

--- a/solution.py
+++ b/solution.py
@@ -45,11 +45,8 @@
     upq_hbm,
     vdw_hbm,
     upv_hbm,
-    down_q_out,
-    up_q_out,
-    down_v_out,
-    up_v_out,
-    dx_hbm,
+    ag_out,
+    dx,
     x,
     q,
     g,
@@ -80,7 +77,6 @@
     rs_src,
     rs_rcv,
     ag,
-    dx,
     loc_sem,
     kv_ssem,
     kv_rsem,
@@ -92,7 +88,6 @@
     t_rsem,
     r_ssem,
     r_rsem,
-    out_sem,
 ):
     c = lax.axis_index("ctx")
     p = lax.axis_index("dp")
@@ -123,7 +118,7 @@
         for which, ref in ((0, k_hbm), (1, v_hbm)):
             for head in range(2):
                 col = (half * 2 + head) * D
-                kv_loads.append(load(ref.at[:, col : col + D], kvw.at[half, 0, which, head]))
+                kv_loads.append(load(ref.at[:, col : col + D], kvw.at[half, 0, head, which]))
     dw_loads = [load(qdw_hbm, dw.at[0:16]), load(vdw_hbm, dw.at[16:32])]
     x_load = load(x_hbm, x)
     q_load = load(q_hbm, q)
@@ -144,29 +139,35 @@
             return carry
 
         lax.fori_loop(1, 16, greet, 0)
-        pl.semaphore_wait(barrier, 30)
+        pl.semaphore_signal(
+            barrier,
+            inc=1,
+            device_id=(lax.rem(c + 8, CTX), lax.rem(p + 8, DP)),
+            device_id_type=MESH,
+        )
+        pl.semaphore_wait(barrier, 31)
 
     lags = (lax.rem(c, 4), lax.rem(c + 2, 4))
     parity = lax.rem(c, 2)
     first_half = lax.rem(c, 4) // 2
     second_half = 1 - first_half
 
-    def kv_copy(half, slot):
+    def kv_copy(half, slot, kv):
         return remote(
-            kvw.at[half, slot],
-            kvw.at[half, slot + 1],
-            kv_ssem.at[half, slot],
-            kv_rsem.at[half, slot + 1],
+            kvw.at[half, slot, kv],
+            kvw.at[half, slot + 1, kv],
+            kv_ssem.at[half, slot, kv],
+            kv_rsem.at[half, slot + 1, kv],
             right,
             p,
         )
 
-    def kv_arrived(half, slot):
+    def kv_arrived(half, slot, kv):
         remote(
-            kvw.at[half, slot],
-            kvw.at[half, slot],
-            kv_ssem.at[half, slot],
-            kv_rsem.at[half, slot],
+            kvw.at[half, slot, kv],
+            kvw.at[half, slot, kv],
+            kv_ssem.at[half, slot, kv],
+            kv_rsem.at[half, slot, kv],
             right,
             p,
         ).wait_recv()
@@ -174,11 +175,8 @@
     with jax.named_scope("kv_send"):
         for copy in kv_loads:
             copy.wait()
-        for half in range(2):
-
-            @pl.when(lags[half] < 3)
-            def _(half=half):
-                kv_copy(half, 0).start()
+        for kv in range(2):
+            kv_copy(first_half, 0, kv).start()
 
     core = lax.rem(p, 2)
     px = lax.rem(p // 2, 4)
@@ -191,42 +189,67 @@
         return yy * 8 + xx * 2 + cc
 
     x_up, x_dn, y_nb, sib = at(0, 1, 0), at(0, -1, 0), at(1, 0, 0), at(0, 0, 1)
-    origin = [at(0, -1, 0), at(0, 1, 0), at(1, 0, 0), at(0, 2, 0), at(1, -1, 0), at(1, 1, 0), at(1, 2, 0)]
-    origin = origin + [at(0, 0, 1)] + [
-        at(0, -1, 1),
-        at(0, 1, 1),
-        at(1, 0, 1),
-        at(0, 2, 1),
-        at(1, -1, 1),
-        at(1, 1, 1),
-        at(1, 2, 1),
+    far = lax.rem(c + 8, CTX)
+    rows = SHARD // 2
+    own, up, dn, opp = p, x_up, x_dn, at(0, 2, 0)
+    y_own, y_up, y_dn, y_opp = at(1, 0, 0), at(1, 1, 0), at(1, -1, 0), at(1, 2, 0)
+    w_plan = [
+        (own, dn, 2, c, x_up),
+        (own, up, 2, c, x_dn),
+        (own, y_own, 0, c, y_nb),
+        (own, y_own, 1, far, y_nb),
+        (own, sib, 2, c, sib),
+        (up, opp, 0, c, x_dn),
+        (dn, opp, 1, c, x_up),
+        (up, y_up, 0, c, y_nb),
+        (dn, y_dn, 0, far, y_nb),
+        (y_own, y_up, 1, c, x_dn),
+        (y_own, y_dn, 1, c, x_up),
+        (opp, y_opp, 0, c, y_nb),
+        (opp, y_opp, 1, far, y_nb),
+        (dn, at(0, -1, 1), 2, c, sib),
+        (up, at(0, 1, 1), 2, c, sib),
+        (y_own, at(1, 0, 1), 2, c, sib),
+        (opp, at(0, 2, 1), 2, c, sib),
+        (y_up, at(1, 1, 1), 2, c, sib),
+        (y_dn, at(1, -1, 1), 2, c, sib),
+        (y_opp, at(1, 2, 1), 2, c, sib),
     ]
 
-    def w_copy(kind, shard, target, src=None):
-        block = w.at[shard]
-        return remote(
-            block if src is None else src, block, w_ssem.at[kind], w_rsem.at[kind], c, target
-        )
-
-    def w_arrived(kind):
-        remote(
-            w.at[origin[kind]], w.at[origin[kind]], w_ssem.at[kind], w_rsem.at[kind], c, sib
-        ).wait_recv()
-
-    w_sends = {
-        0: w_copy(0, p, x_up, w_hbm),
-        1: w_copy(1, p, x_dn, w_hbm),
-        2: w_copy(2, p, y_nb, w_hbm),
-        7: w_copy(7, p, sib, w_hbm),
-        3: w_copy(3, origin[1], x_dn),
-        4: w_copy(4, origin[2], x_up),
-        5: w_copy(5, origin[1], y_nb),
-        6: w_copy(6, origin[3], y_nb),
-    }
-    for i in range(7):
-        w_sends[8 + i] = w_copy(8 + i, origin[i], sib)
-    for kind in (0, 1, 2, 7):
-        w_sends[kind].start()
+    def w_part(shard, part):
+        return w.at[shard] if part == 2 else w.at[shard, part * rows : (part + 1) * rows]
+
+    def w_copy(number):
+        shard, _, part, ctx, target = w_plan[number]
+        block = w_part(shard, part)
+        src = block
+        if number < 5:
+            src = w_hbm if part == 2 else w_hbm.at[part * rows : (part + 1) * rows]
+        return remote(src, block, w_ssem.at[number], w_rsem.at[number], ctx, target)
+
+    def w_arrived(*numbers):
+        for number in numbers:
+            _, shard, part, ctx, target = w_plan[number]
+            block = w_part(shard, part)
+            remote(
+                block, block, w_ssem.at[number], w_rsem.at[number], ctx, target
+            ).wait_recv()
+
+    def w_start(*numbers):
+        for number in numbers:
+            w_copy(number).start()
+
+    def w_round_1():
+        with jax.named_scope("w_round_1"):
+            w_arrived(0, 1, 2, 3)
+            w_start(5, 6, 7, 8, 9, 10, 13, 14, 15)
+
+    def w_round_2():
+        with jax.named_scope("w_round_2"):
+            w_arrived(5, 6)
+            w_start(11, 12, 16)
+
+    w_start(2, 3, 0, 1, 4)
 
     with jax.named_scope("bias"):
         row = lax.broadcasted_iota(jnp.int32, (T, LANES), 0)
@@ -258,37 +281,28 @@
         ht4[32:48, 384:640] = padded.astype(BF16)
         ht4[48:64, 512:768] = turned.astype(BF16)
 
-    with jax.named_scope("kv_forward_1"):
-        for half in range(2):
-
-            @pl.when(lags[half] >= 1)
-            def _(half=half):
-                kv_arrived(half, 1)
-
-            @pl.when((lags[half] >= 1) & (lags[half] <= 2))
-            def _(half=half):
-                kv_copy(half, 1).start()
-
-        q_load.wait()
-        g_load.wait()
+    q_load.wait()
+    g_load.wait()
 
     def four_heads(ref, quad):
         block = ref[:, pl.ds(pl.multiple_of(quad * 512, 512), 512)]
         return jnp.concatenate([block[:, i * D : (i + 1) * D] for i in range(4)], axis=0)
 
-    def attend(half, kv, nk):
+    def attend(half, kv, nk, between=None):
         n = nk * T
 
-        keys = kvw[half, 0:nk, 0, kv].reshape(n, D)
+        keys = kvw[half, 0:nk, kv, 0].reshape(n, D)
         kt[:, 0:n] = keys.T
         dv_acc[0:n] = jnp.zeros((n, D), F32)
 
         def quad_step(i, carry):
+            if between is not None:
+                pl.when(i == 1)(between)
             quad = half * 4 + kv * 2 + i
             q4 = four_heads(q, quad)
             top = None
             for d in range(nk):
-                s = nt(kvw[half, d, 0, kv], q4)
+                s = nt(kvw[half, d, kv, 0], q4)
                 if d == 0:
                     s = s + bias[...]
                 s_buf[d * T : (d + 1) * T] = s
@@ -296,7 +310,7 @@
                 top = m if top is None else jnp.maximum(top, m)
             g4 = four_heads(g, quad)
             for d in range(nk):
-                dp_buf[d * T : (d + 1) * T] = nt(kvw[half, d, 1, kv], g4)
+                dp_buf[d * T : (d + 1) * T] = nt(kvw[half, d, kv, 1], g4)
 
             def exp_step(j, sums):
                 rows = pl.ds(pl.multiple_of(j * CHUNK, CHUNK), CHUNK)
@@ -340,59 +354,66 @@
             p,
         )
 
-    def first_step(kv, carry):
-        @pl.when(parity == 0)
-        def _():
+    @pl.when(parity == 0)
+    def _():
+        def first_step(kv, carry):
             attend(first_half, kv, 1)
 
-        @pl.when(parity == 1)
-        def _():
+            @pl.when(kv == 0)
+            def _():
+                kv_copy(second_half, 0, 0).start()
+
+            return carry
+
+        with jax.named_scope("even_first"):
+            lax.fori_loop(0, 2, first_step, 0)
+        with jax.named_scope("even_pass"):
+            kv_arrived(second_half, 1, 0)
+            kv_copy(second_half, 1, 0).start()
+            kv_arrived(second_half, 2, 0)
+            kv_copy(second_half, 2, 0).start()
+            kv_copy(second_half, 0, 1).start()
+            kv_arrived(second_half, 1, 1)
+            kv_copy(second_half, 1, 1).start()
+
+        def second_step(kv, carry):
+            @pl.when(kv == 1)
+            def _():
+                kv_arrived(second_half, 2, 1)
+                kv_copy(second_half, 2, 1).start()
+                w_round_1()
+
+            attend(second_half, kv, 3)
+            return carry
+
+        with jax.named_scope("even_second"):
+            lax.fori_loop(0, 2, second_step, 0)
+        w_round_2()
+
+    @pl.when(parity == 1)
+    def _():
+        def first_step(kv, carry):
+            kv_arrived(first_half, 1, kv)
+            kv_copy(first_half, 1, kv).start()
             attend(first_half, kv, 2)
-
-        return carry
-
-    with jax.named_scope("attend_first"):
-        lax.fori_loop(0, 2, first_step, 0)
-
-    with jax.named_scope("kv_forward_2"):
-        kv_arrived(second_half, 2)
-
-        @pl.when(parity == 0)
-        def _():
-            kv_copy(second_half, 2).start()
-
-    with jax.named_scope("w_forward_1"):
-        for kind in (0, 1, 2):
-            w_arrived(kind)
-        for kind in (3, 4, 5, 8, 9, 10):
-            w_sends[kind].start()
-
-    with jax.named_scope("kv_last"):
-        @pl.when(parity == 1)
-        def _():
-            kv_arrived(second_half, 3)
-
-    def second_step(kv, carry):
-        @pl.when(parity == 0)
-        def _():
-            attend(second_half, kv, 3)
-
-        @pl.when(parity == 1)
-        def _():
-            attend(second_half, kv, 4)
-
-        @pl.when(kv == 0)
-        def _():
-            with jax.named_scope("w_forward_2"):
-                for kind in (3, 4, 5):
-                    w_arrived(kind)
-                for kind in (6, 11, 12, 13):
-                    w_sends[kind].start()
-
-        return carry
-
-    with jax.named_scope("attend_second"):
-        lax.fori_loop(0, 2, second_step, 0)
+            return carry
+
+        with jax.named_scope("odd_first"):
+            lax.fori_loop(0, 2, first_step, 0)
+
+        def second_step(kv, carry):
+            for slot in (1, 2, 3):
+                kv_arrived(second_half, slot, kv)
+
+            def between():
+                pl.when(kv == 0)(w_round_1)
+                pl.when(kv == 1)(w_round_2)
+
+            attend(second_half, kv, 4, between)
+            return carry
+
+        with jax.named_scope("odd_second"):
+            lax.fori_loop(0, 2, second_step, 0)
 
     with jax.named_scope("query_terms"):
         for copy in up_loads:
@@ -430,7 +451,7 @@
             term[i, :, 0:SHARD] = nn(code, x[:, cols]).astype(BF16)
             return carry
 
-        lax.fori_loop(0, DP, step, 0)
+        lax.fori_loop(0, DP, step, 0, unroll=4)
 
     def term_copy(which, off):
         target = lax.rem(p + off, DP)
@@ -456,9 +477,11 @@
         each(lambda off: term_copy(0, off).start())
         rcv_q[0] = term_q[p]
 
-    with jax.named_scope("w_forward_3"):
-        w_arrived(6)
-        w_sends[14].start()
+    with jax.named_scope("w_round_3"):
+        w_arrived(7, 8, 9, 10)
+        w_start(17, 18)
+        w_arrived(11, 12)
+        w_start(19)
 
     with jax.named_scope("value_gradient"):
         for half in range(2):
@@ -488,23 +511,17 @@
 
     with jax.named_scope("w_wait"):
         w_load.wait()
-        for kind in range(7, 15):
-            w_arrived(kind)
+        w_arrived(4, *range(13, 20))
         code = (ADAPTER_SCALE * codes[...].astype(BF16).astype(F32)).T
         code = code[0:T, :].astype(BF16)
-
-    def out_copy(i):
-        cols = pl.ds(pl.multiple_of(i * SHARD, SHARD), SHARD)
-        return pltpu.make_async_copy(dx.at[:, cols], dx_hbm.at[:, cols], out_sem.at[i])
 
     def dx_step(i, carry):
         cols = pl.ds(pl.multiple_of(i * SHARD, SHARD), SHARD)
         dx[:, cols] = (nt(gv[...], w[i]) + nn(code, dw[:, cols])).astype(BF16)
-        out_copy(i).start()
         return carry
 
     with jax.named_scope("dx_1"):
-        lax.fori_loop(0, 8, dx_step, 0)
+        lax.fori_loop(0, 8, dx_step, 0, unroll=2)
 
     with jax.named_scope("sum_dp"):
         each(lambda off: term_copy(0, off).wait_recv())
@@ -535,7 +552,7 @@
     rs_rcv[0] = rs_src[c]
 
     with jax.named_scope("dx_2"):
-        lax.fori_loop(8, 12, dx_step, 0)
+        lax.fori_loop(8, 12, dx_step, 0, unroll=2)
 
     with jax.named_scope("sum_ctx"):
         each(lambda off: row_copy(off).wait_recv())
@@ -544,38 +561,28 @@
         each(lambda off: sum_copy(off).start())
 
     with jax.named_scope("dx_3"):
-        lax.fori_loop(12, 16, dx_step, 0)
+        lax.fori_loop(12, 16, dx_step, 0, unroll=2)
 
     with jax.named_scope("outputs"):
         each(sum_arrived)
-        for j in range(4):
-            down_q_out[:, j * D : (j + 1) * D] = ag[:, j, :]
-            down_v_out[:, j * D : (j + 1) * D] = ag[:, 6 + j, :]
-        for j in range(2):
-            up_q_out[:, j * D : (j + 1) * D] = ag[:, 4 + j, :]
-        piece = ag[:, 10, :]
-        for j in range(4):
-
-            @pl.when(lax.rem(p, 4) == j)
-            def _(j=j):
-                up_v_out[...] = piece[:, 32 * j : 32 * (j + 1)]
+        ag_out[...] = ag[...]
 
     with jax.named_scope("drain"):
-        def out_wait(i, carry):
-            out_copy(i).wait()
-            return carry
-
-        lax.fori_loop(0, DP, out_wait, 0)
+        for kv in range(2):
+            kv_copy(first_half, 0, kv).wait_send()
+
+        @pl.when(parity == 0)
+        def _():
+            for slot in range(3):
+                for kv in range(2):
+                    kv_copy(second_half, slot, kv).wait_send()
+
+        @pl.when(parity == 1)
+        def _():
+            for kv in range(2):
+                kv_copy(first_half, 1, kv).wait_send()
+
         for half in range(2):
-
-            @pl.when(lags[half] < 3)
-            def _(half=half):
-                kv_copy(half, 0).wait_send()
-
-            @pl.when((lags[half] >= 1) & (lags[half] <= 2))
-            def _(half=half):
-                kv_copy(half, 1).wait_send()
-
             for d in range(1, 4):
 
                 @pl.when(lags[half] >= d)
@@ -583,12 +590,8 @@
                     for kv in range(2):
                         dv_copy(half, d, kv).wait_send()
 
-        @pl.when(parity == 0)
-        def _():
-            kv_copy(second_half, 2).wait_send()
-
-        for kind in range(15):
-            w_sends[kind].wait_send()
+        for number in range(20):
+            w_copy(number).wait_send()
 
         def sent(off):
             term_copy(0, off).wait_send()
@@ -597,6 +600,55 @@
             sum_copy(off).wait_send()
 
         each(sent)
+
+
+def place(sums, dx, down_q_out, up_q_out, down_v_out, up_v_out, dx_out, wide, narrow, sem):
+    p = lax.axis_index("dp")
+    copies = [pltpu.make_async_copy(dx, dx_out.at[0], sem.at[0])]
+    copies[0].start()
+    for j in range(11):
+        wide[:, j * D : (j + 1) * D] = sums[:, j, :]
+    piece = sums[:, 10, :]
+    for j in range(4):
+
+        @pl.when(lax.rem(p, 4) == j)
+        def _(j=j):
+            narrow[...] = piece[:, 32 * j : 32 * (j + 1)]
+
+    for src, dst in (
+        (wide.at[:, 0:512], down_q_out),
+        (wide.at[:, 512:768], up_q_out),
+        (wide.at[:, 768:1280], down_v_out),
+        (narrow, up_v_out),
+    ):
+        copies.append(pltpu.make_async_copy(src, dst, sem.at[len(copies)]))
+        copies[-1].start()
+    for copy in copies:
+        copy.wait()
+
+
+def deliver(sums, dx):
+    return pl.pallas_call(
+        place,
+        out_shape=(
+            jax.ShapeDtypeStruct((16, SHARD), F32),
+            jax.ShapeDtypeStruct((16, DQ // DP), F32),
+            jax.ShapeDtypeStruct((16, SHARD), F32),
+            jax.ShapeDtypeStruct((16, DKV // DP), F32),
+            jax.ShapeDtypeStruct((1, T, WIDTH), BF16),
+        ),
+        in_specs=[pl.BlockSpec(memory_space=pltpu.VMEM)] * 2,
+        out_specs=[pl.BlockSpec(memory_space=pl.ANY)] * 5,
+        scratch_shapes=[
+            pltpu.VMEM((16, 11 * D), F32),
+            pltpu.VMEM((16, DKV // DP), F32),
+            pltpu.SemaphoreType.DMA((5,)),
+        ],
+        compiler_params=pltpu.CompilerParams(vmem_limit_bytes=16 * 1024 * 1024),
+    )(
+        pltpu.with_memory_space_constraint(sums, pltpu.VMEM),
+        pltpu.with_memory_space_constraint(dx, pltpu.VMEM),
+    )
 
 
 def on_device(
@@ -611,18 +663,14 @@
     value_down_weight,
     up_v,
 ):
-    out = pl.pallas_call(
+    sums, dx = pl.pallas_call(
         kernel,
         out_shape=(
-            jax.ShapeDtypeStruct((16, SHARD), F32),
-            jax.ShapeDtypeStruct((16, DQ // DP), F32),
-            jax.ShapeDtypeStruct((16, SHARD), F32),
-            jax.ShapeDtypeStruct((16, DKV // DP), F32),
-            jax.ShapeDtypeStruct((T, WIDTH), BF16),
+            pltpu.VMEM((CTX, 16, D), F32),
+            pltpu.VMEM((T, WIDTH), BF16),
         ),
         in_specs=[pl.BlockSpec(memory_space=pl.ANY)] * 10,
-        out_specs=[pl.BlockSpec(memory_space=pltpu.VMEM)] * 4
-        + [pl.BlockSpec(memory_space=pl.ANY)],
+        out_specs=[pl.BlockSpec(memory_space=pltpu.VMEM)] * 2,
         scratch_shapes=[
             pltpu.VMEM((T, WIDTH), BF16),
             pltpu.VMEM((T, DQ), BF16),
@@ -654,36 +702,39 @@
             pltpu.VMEM((CTX, 16, D), F32),
             pltpu.VMEM((CTX, 16, D), F32),
             pltpu.VMEM((CTX, 16, D), F32),
-            pltpu.VMEM((T, WIDTH), BF16),
             pltpu.SemaphoreType.DMA((16,)),
-            pltpu.SemaphoreType.DMA((2, 4)),
-            pltpu.SemaphoreType.DMA((2, 4)),
-            pltpu.SemaphoreType.DMA((15,)),
-            pltpu.SemaphoreType.DMA((15,)),
+            pltpu.SemaphoreType.DMA((2, 4, 2)),
+            pltpu.SemaphoreType.DMA((2, 4, 2)),
+            pltpu.SemaphoreType.DMA((20,)),
+            pltpu.SemaphoreType.DMA((20,)),
             pltpu.SemaphoreType.DMA((2, 3, 2)),
             pltpu.SemaphoreType.DMA((2, 3, 2)),
             pltpu.SemaphoreType.DMA((2, 16)),
             pltpu.SemaphoreType.DMA((2, 16)),
             pltpu.SemaphoreType.DMA((2, 16)),
             pltpu.SemaphoreType.DMA((2, 16)),
-            pltpu.SemaphoreType.DMA((16,)),
         ],
         compiler_params=pltpu.CompilerParams(
-            collective_id=0, has_side_effects=True, vmem_limit_bytes=56 * 1024 * 1024
+            collective_id=0, has_side_effects=True, vmem_limit_bytes=44 * 1024 * 1024
         ),
     )(
-        inputs[0],
-        query_saved[0],
-        key_saved[0],
-        value_saved[0],
-        grad_out[0],
-        value_weight,
-        query_down_weight,
-        up_q,
-        value_down_weight,
-        up_v,
+        *(
+            pltpu.with_memory_space_constraint(operand, pltpu.HBM)
+            for operand in (
+                inputs[0],
+                query_saved[0],
+                key_saved[0],
+                value_saved[0],
+                grad_out[0],
+                value_weight,
+                query_down_weight,
+                up_q,
+                value_down_weight,
+                up_v,
+            )
+        )
     )
-    return out[0], out[1], out[2], out[3], out[4][None]
+    return deliver(sums, dx)
 
 
 def solution(mesh):

time: 95.5 us -> 72.6 us (0.76)
  Pallas kernels: 85.3 us -> 71.9 us
  local copies, waits for them, and re-layouts: 9.22 us -> 0 us
    pallas_call x1 -> x2, Pallas kernels: 85.3 us -> 71.9 us  [the longest x1 70.1 us: on_device(): pl.pallas_call(kernel, out_shape=(pltpu.VMEM((CTX, 16, D), F32), pltpu.VM...]
    unnamed x5 -> x0, local copies, waits for them, and re-layouts: 9.22 us -> none
where the time goes in v2:
time: 72.6 us; the launch traced here: 72.5 us
  Pallas kernels  71.9 us (99%)
    pallas_call x1, Pallas kernels, on_device(): pl.pallas_call(kernel, out_shape=(pltpu.VMEM((CTX, 16, D), F32), pltpu.VM...  70.1 us
    pallas_call x1, Pallas kernels, deliver(): pl.pallas_call(place, out_shape=(jax.ShapeDtypeStruct((16, SHARD), F32),...  1.72 us

profile of v2, /device:TPU:1, one launch (start us, length us, event | category | flops | bytes accessed | tf_op | source)
XLA Modules:
  0.0 72.5 jit_solution(14980252930538425033)
XLA Ops:
  0.6 70.1 %shard_map.137 = (f32[16,16,128]{2,1,0:T(8,128)S(1)}, bf16[192,8192]{1,0:T(8,128)(2,1)S(1)}) custom-call(bf16[192,8192]{1,0:T(8,128)(2,1)} %bitcast.5, bf16[192,4096]{1,0:T(8,128)(2,1)} %bitcast.6, bf16[192,512]{1,0:T(8,128)(2,1)} %bitcast.8, bf16[192,512]{1,0:T(8,128)(2,1)} %bitcast.9, bf16[192,4096]{1,0:T(8,128)(2,1)} %bitcast.7, bf16[512,512]{1,0:T(8,128)(2,1)} %w_hbm.1, ...), custom_call_target="tpu_custom_call" | custom-call | tf_op jit(solution)/shard_map/pallas_call | solution.py:666
  70.8 1.7 %shard_map.138 = (f32[16,512]{1,0:T(8,128)}, f32[16,256]{1,0:T(8,128)}, f32[16,512]{1,0:T(8,128)}, f32[16,32]{1,0:T(8,128)}, bf16[1,192,8192]{2,1,0:T(8,128)(2,1)}) custom-call(f32[16,16,128]{2,1,0:T(8,128)S(1)} %get-tuple-element.7.sums, bf16[192,8192]{1,0:T(8,128)(2,1)S(1)} %get-tuple-element.8.dx), custom_call_target="tpu_custom_call" | custom-call | tf_op jit(solution)/shard_map/pallas_call | solution.py:631

commit v3 on v2

--- a/solution.py
+++ b/solution.py
@@ -138,7 +138,7 @@
             )
             return carry
 
-        lax.fori_loop(1, 16, greet, 0)
+        lax.fori_loop(1, 16, greet, 0, unroll=True)
         pl.semaphore_signal(
             barrier,
             inc=1,
@@ -290,55 +290,75 @@
 
     def attend(half, kv, nk, between=None):
         n = nk * T
-
         keys = kvw[half, 0:nk, kv, 0].reshape(n, D)
         kt[:, 0:n] = keys.T
-        dv_acc[0:n] = jnp.zeros((n, D), F32)
-
-        def quad_step(i, carry):
-            if between is not None:
-                pl.when(i == 1)(between)
-            quad = half * 4 + kv * 2 + i
-            q4 = four_heads(q, quad)
+        quads = [half * 4 + kv * 2 + i for i in range(2)]
+        tops, invs, deltas = {}, {}, {}
+
+        def scores(i):
+            q4 = four_heads(q, quads[i])
             top = None
             for d in range(nk):
                 s = nt(kvw[half, d, kv, 0], q4)
                 if d == 0:
                     s = s + bias[...]
-                s_buf[d * T : (d + 1) * T] = s
+                s_buf[i, d * T : (d + 1) * T] = s
                 m = jnp.max(s, axis=0, keepdims=True)
                 top = m if top is None else jnp.maximum(top, m)
-            g4 = four_heads(g, quad)
+            tops[i] = top
+
+        def values(i):
+            g4 = four_heads(g, quads[i])
             for d in range(nk):
-                dp_buf[d * T : (d + 1) * T] = nt(kvw[half, d, kv, 1], g4)
+                dp_buf[i, d * T : (d + 1) * T] = nt(kvw[half, d, kv, 1], g4)
+
+        def weigh(i):
+            values(i)
+            top = tops[i]
 
             def exp_step(j, sums):
                 rows = pl.ds(pl.multiple_of(j * CHUNK, CHUNK), CHUNK)
-                e = jnp.exp2((s_buf[rows] - top) * exp2_scale)
-                s_buf[rows] = e
+                e = jnp.exp2((s_buf[i, rows] - top) * exp2_scale)
+                s_buf[i, rows] = e
                 return (
                     sums[0] + jnp.sum(e.reshape(CHUNK // 8, 8, LANES), axis=0),
-                    sums[1] + jnp.sum((e * dp_buf[rows]).reshape(CHUNK // 8, 8, LANES), axis=0),
+                    sums[1]
+                    + jnp.sum((e * dp_buf[i, rows]).reshape(CHUNK // 8, 8, LANES), axis=0),
                 )
 
             zero = jnp.zeros((8, LANES), F32)
             total, weighted = lax.fori_loop(0, n // CHUNK, exp_step, (zero, zero), unroll=True)
-            inv = 1.0 / jnp.sum(total, axis=0, keepdims=True)
-            delta = jnp.sum(weighted, axis=0, keepdims=True) * inv
+            invs[i] = 1.0 / jnp.sum(total, axis=0, keepdims=True)
+            deltas[i] = jnp.sum(weighted, axis=0, keepdims=True) * invs[i]
+
+        def grads(i):
+            inv, delta = invs[i], deltas[i]
 
             def grad_step(j, carry):
                 rows = pl.ds(pl.multiple_of(j * CHUNK, CHUNK), CHUNK)
-                probs = s_buf[rows] * inv
-                pb_buf[rows] = probs.astype(BF16)
-                ds_buf[rows] = (probs * (dp_buf[rows] - delta)).astype(BF16)
+                probs = s_buf[i, rows] * inv
+                pb_buf[i, rows] = probs.astype(BF16)
+                ds_buf[i, rows] = (probs * (dp_buf[i, rows] - delta)).astype(BF16)
                 return carry
 
             lax.fori_loop(0, n // CHUNK, grad_step, 0, unroll=True)
-            dv_acc[0:n] += nn(pb_buf[0:n], g4)
-            gq[quad] = (nn(kt[:, 0:n], ds_buf[0:n]) * scale).astype(BF16)
-            return carry
-
-        lax.fori_loop(0, 2, quad_step, 0)
+
+        def products(i):
+            g4 = four_heads(g, quads[i])
+            dv = nn(pb_buf[i, 0:n], g4)
+            if i == 0:
+                dv_acc[0:n] = dv
+            else:
+                dv_acc[0:n] += dv
+            gq[quads[i]] = (nn(kt[:, 0:n], ds_buf[i, 0:n]) * scale).astype(BF16)
+
+        for i in range(2):
+            scores(i)
+            if i == 0 and between is not None:
+                between()
+            weigh(i)
+            grads(i)
+            products(i)
         dv_own[half, kv] = dv_acc[0:T]
         for d in range(1, nk):
             dv_snd[half, d - 1, kv] = dv_acc[d * T : (d + 1) * T].astype(BF16)
@@ -388,7 +408,6 @@
 
         with jax.named_scope("even_second"):
             lax.fori_loop(0, 2, second_step, 0)
-        w_round_2()
 
     @pl.when(parity == 1)
     def _():
@@ -407,7 +426,6 @@
 
             def between():
                 pl.when(kv == 0)(w_round_1)
-                pl.when(kv == 1)(w_round_2)
 
             attend(second_half, kv, 4, between)
             return carry
@@ -470,18 +488,14 @@
             fn(off)
             return carry
 
-        lax.fori_loop(1, 16, step, 0)
+        lax.fori_loop(1, 16, step, 0, unroll=True)
 
     with jax.named_scope("query_down"):
         down_terms(term_q, code_qt)
         each(lambda off: term_copy(0, off).start())
         rcv_q[0] = term_q[p]
 
-    with jax.named_scope("w_round_3"):
-        w_arrived(7, 8, 9, 10)
-        w_start(17, 18)
-        w_arrived(11, 12)
-        w_start(19)
+    w_round_2()
 
     with jax.named_scope("value_gradient"):
         for half in range(2):
@@ -509,28 +523,31 @@
         each(lambda off: term_copy(1, off).start())
         rcv_v[0] = term_v[p]
 
-    with jax.named_scope("w_wait"):
+    with jax.named_scope("w_round_3"):
+        w_arrived(7, 8, 9, 10)
+        w_start(17, 18)
+
+    def input_gradient():
         w_load.wait()
         w_arrived(4, *range(13, 20))
         code = (ADAPTER_SCALE * codes[...].astype(BF16).astype(F32)).T
         code = code[0:T, :].astype(BF16)
 
-    def dx_step(i, carry):
-        cols = pl.ds(pl.multiple_of(i * SHARD, SHARD), SHARD)
-        dx[:, cols] = (nt(gv[...], w[i]) + nn(code, dw[:, cols])).astype(BF16)
-        return carry
-
-    with jax.named_scope("dx_1"):
-        lax.fori_loop(0, 8, dx_step, 0, unroll=2)
+        def step(i, carry):
+            cols = pl.ds(pl.multiple_of(i * SHARD, SHARD), SHARD)
+            dx[:, cols] = (nt(gv[...], w[i]) + nn(code, dw[:, cols])).astype(BF16)
+            return carry
+
+        lax.fori_loop(0, DP, step, 0, unroll=2)
 
     with jax.named_scope("sum_dp"):
         each(lambda off: term_copy(0, off).wait_recv())
-        each(lambda off: term_copy(1, off).wait_recv())
+        sum_q = jnp.sum(rcv_q[...].astype(F32), axis=0)
         rs_src[...] = jnp.zeros_like(rs_src)
-        sum_q = jnp.sum(rcv_q[...].astype(F32), axis=0)
-        sum_v = jnp.sum(rcv_v[...].astype(F32), axis=0)
         for j in range(6):
             rs_src[:, j, :] = sum_q[:, j * D : (j + 1) * D]
+        each(lambda off: term_copy(1, off).wait_recv())
+        sum_v = jnp.sum(rcv_v[...].astype(F32), axis=0)
         for j in range(5):
             rs_src[:, 6 + j, :] = sum_v[:, j * D : (j + 1) * D]
 
@@ -540,7 +557,7 @@
             rs_src.at[target], rs_rcv.at[off], r_ssem.at[0, off], r_rsem.at[0, off], target, p
         )
 
-    def sum_copy(off, src=None):
+    def sum_copy(off):
         target = lax.rem(c + off, CTX)
         return remote(ag.at[c], ag.at[c], r_ssem.at[1, off], r_rsem.at[1, off], target, p)
 
@@ -550,19 +567,20 @@
 
     each(lambda off: row_copy(off).start())
     rs_rcv[0] = rs_src[c]
-
-    with jax.named_scope("dx_2"):
-        lax.fori_loop(8, 12, dx_step, 0, unroll=2)
-
+    w_arrived(11, 12)
+    w_start(19)
+
+    z = lax.rem(c, 8)
+    early = (z <= 2) | (z >= 6)
+    with jax.named_scope("dx_early"):
+        pl.when(early)(input_gradient)
     with jax.named_scope("sum_ctx"):
         each(lambda off: row_copy(off).wait_recv())
         gradient_scale = ADAPTER_SCALE / math.sqrt(DP * CTX * T)
         ag[c] = jnp.sum(rs_rcv[...], axis=0) * gradient_scale
         each(lambda off: sum_copy(off).start())
-
-    with jax.named_scope("dx_3"):
-        lax.fori_loop(12, 16, dx_step, 0, unroll=2)
-
+    with jax.named_scope("dx_late"):
+        pl.when(jnp.logical_not(early))(input_gradient)
     with jax.named_scope("outputs"):
         each(sum_arrived)
         ag_out[...] = ag[...]
@@ -681,10 +699,10 @@
             pltpu.VMEM((16, DQ), BF16),
             pltpu.VMEM((16, DKV), BF16),
             pltpu.VMEM((T, LANES), F32),
-            pltpu.VMEM((4 * T, LANES), F32),
-            pltpu.VMEM((4 * T, LANES), F32),
-            pltpu.VMEM((4 * T, LANES), BF16),
-            pltpu.VMEM((4 * T, LANES), BF16),
+            pltpu.VMEM((2, 4 * T, LANES), F32),
+            pltpu.VMEM((2, 4 * T, LANES), F32),
+            pltpu.VMEM((2, 4 * T, LANES), BF16),
+            pltpu.VMEM((2, 4 * T, LANES), BF16),
             pltpu.VMEM((D, 4 * T), BF16),
             pltpu.VMEM((4 * T, D), F32),
             pltpu.VMEM((2, 2, T, D), F32),
@@ -715,7 +733,7 @@
             pltpu.SemaphoreType.DMA((2, 16)),
         ],
         compiler_params=pltpu.CompilerParams(
-            collective_id=0, has_side_effects=True, vmem_limit_bytes=44 * 1024 * 1024
+            collective_id=0, has_side_effects=True, vmem_limit_bytes=52 * 1024 * 1024
         ),
     )(
         *(

time: 72.6 us -> 67.9 us (0.935)
  Pallas kernels: 71.9 us -> 67.2 us
    pallas_call x1, Pallas kernels: 70.1 us -> 65.5 us  [on_device(): pl.pallas_call(kernel, out_shape=(pltpu.VMEM((CTX, 16, D), F32), pltpu.VM...]
where the time goes in v3:
time: 67.9 us; the launch traced here: 67.8 us
  Pallas kernels  67.2 us (99%)
    pallas_call x1, Pallas kernels, on_device(): pl.pallas_call(kernel, out_shape=(pltpu.VMEM((CTX, 16, D), F32), pltpu.VM...  65.5 us
    pallas_call x1, Pallas kernels, deliver(): pl.pallas_call(place, out_shape=(jax.ShapeDtypeStruct((16, SHARD), F32),...  1.72 us

profile of v3, /device:TPU:1, one launch (start us, length us, event | category | flops | bytes accessed | tf_op | source)
XLA Modules:
  0.0 67.8 jit_solution(13764909595174138720)
XLA Ops:
  0.6 65.5 %shard_map.137 = (f32[16,16,128]{2,1,0:T(8,128)S(1)}, bf16[192,8192]{1,0:T(8,128)(2,1)S(1)}) custom-call(bf16[192,8192]{1,0:T(8,128)(2,1)} %bitcast.5, bf16[192,4096]{1,0:T(8,128)(2,1)} %bitcast.6, bf16[192,512]{1,0:T(8,128)(2,1)} %bitcast.8, bf16[192,512]{1,0:T(8,128)(2,1)} %bitcast.9, bf16[192,4096]{1,0:T(8,128)(2,1)} %bitcast.7, bf16[512,512]{1,0:T(8,128)(2,1)} %w_hbm.1, ...), custom_call_target="tpu_custom_call" | custom-call | tf_op jit(solution)/shard_map/pallas_call | solution.py:684
  66.1 1.7 %shard_map.138 = (f32[16,512]{1,0:T(8,128)}, f32[16,256]{1,0:T(8,128)}, f32[16,512]{1,0:T(8,128)}, f32[16,32]{1,0:T(8,128)}, bf16[1,192,8192]{2,1,0:T(8,128)(2,1)}) custom-call(f32[16,16,128]{2,1,0:T(8,128)S(1)} %get-tuple-element.7.sums, bf16[192,8192]{1,0:T(8,128)(2,1)S(1)} %get-tuple-element.8.dx), custom_call_target="tpu_custom_call" | custom-call | tf_op jit(solution)/shard_map/pallas_call | solution.py:649

commit v4 on v2

--- a/solution.py
+++ b/solution.py
@@ -24,6 +24,7 @@
 DKV = 512
 ADAPTER_SCALE = 2.0
 CHUNK = 32
+FAR_FIRST = (4, 12, 3, 5, 11, 13, 2, 6, 10, 14, 1, 7, 9, 15, 8)
 
 
 def nt(a, b):
@@ -119,13 +120,6 @@
             for head in range(2):
                 col = (half * 2 + head) * D
                 kv_loads.append(load(ref.at[:, col : col + D], kvw.at[half, 0, head, which]))
-    dw_loads = [load(qdw_hbm, dw.at[0:16]), load(vdw_hbm, dw.at[16:32])]
-    x_load = load(x_hbm, x)
-    q_load = load(q_hbm, q)
-    g_load = load(g_hbm, g)
-    up_loads = [load(upq_hbm, upq), load(upv_hbm, upv)]
-    w_load = load(w_hbm, w.at[p])
-
     with jax.named_scope("greet"):
         barrier = pltpu.get_barrier_semaphore()
 
@@ -138,13 +132,19 @@
             )
             return carry
 
-        lax.fori_loop(1, 16, greet, 0)
+        lax.fori_loop(1, 16, greet, 0, unroll=True)
         pl.semaphore_signal(
             barrier,
             inc=1,
             device_id=(lax.rem(c + 8, CTX), lax.rem(p + 8, DP)),
             device_id_type=MESH,
         )
+        q_load = load(q_hbm, q)
+        g_load = load(g_hbm, g)
+        dw_loads = [load(qdw_hbm, dw.at[0:16]), load(vdw_hbm, dw.at[16:32])]
+        x_load = load(x_hbm, x)
+        up_loads = [load(upq_hbm, upq), load(upv_hbm, upv)]
+        w_load = load(w_hbm, w.at[p])
         pl.semaphore_wait(barrier, 31)
 
     lags = (lax.rem(c, 4), lax.rem(c + 2, 4))
@@ -177,6 +177,10 @@
             copy.wait()
         for kv in range(2):
             kv_copy(first_half, 0, kv).start()
+
+        @pl.when(parity == 0)
+        def _():
+            kv_copy(second_half, 0, 0).start()
 
     core = lax.rem(p, 2)
     px = lax.rem(p // 2, 4)
@@ -261,25 +265,10 @@
         )
         bias[...] = jnp.where(row <= lane - turn * T, 0.0, -jnp.inf).astype(F32)
 
-    with jax.named_scope("hidden"):
-        for copy in dw_loads:
-            copy.wait()
-        x_load.wait()
-
-        def hidden_step(i, acc):
-            cols = pl.ds(pl.multiple_of(i * 1024, 1024), 1024)
-            return acc + nt(dw[:, cols], x[:, cols])
-
-        hidden = lax.fori_loop(0, 8, hidden_step, jnp.zeros((32, T), F32))
-        hid[...] = jnp.zeros_like(hid)
-        hid[:, 0:T] = hidden.astype(BF16).astype(F32)
-        ht4[...] = jnp.zeros_like(ht4)
-        padded = hid[0:16, :]
-        turned = pltpu.roll(padded, 64, 1)
-        ht4[0:16, 0:256] = padded.astype(BF16)
-        ht4[16:32, 128:384] = turned.astype(BF16)
-        ht4[32:48, 384:640] = padded.astype(BF16)
-        ht4[48:64, 512:768] = turned.astype(BF16)
+    @pl.when(parity == 0)
+    def _():
+        kv_arrived(second_half, 1, 0)
+        kv_copy(second_half, 1, 0).start()
 
     q_load.wait()
     g_load.wait()
@@ -288,7 +277,7 @@
         block = ref[:, pl.ds(pl.multiple_of(quad * 512, 512), 512)]
         return jnp.concatenate([block[:, i * D : (i + 1) * D] for i in range(4)], axis=0)
 
-    def attend(half, kv, nk, between=None):
+    def attend(half, kv, nk):
         n = nk * T
 
         keys = kvw[half, 0:nk, kv, 0].reshape(n, D)
@@ -296,8 +285,6 @@
         dv_acc[0:n] = jnp.zeros((n, D), F32)
 
         def quad_step(i, carry):
-            if between is not None:
-                pl.when(i == 1)(between)
             quad = half * 4 + kv * 2 + i
             q4 = four_heads(q, quad)
             top = None
@@ -354,6 +341,26 @@
             p,
         )
 
+    def hidden_layers():
+        for copy in dw_loads:
+            copy.wait()
+        x_load.wait()
+
+        def hidden_step(i, acc):
+            cols = pl.ds(pl.multiple_of(i * 1024, 1024), 1024)
+            return acc + nt(dw[:, cols], x[:, cols])
+
+        hidden = lax.fori_loop(0, 8, hidden_step, jnp.zeros((32, T), F32))
+        hid[...] = jnp.zeros_like(hid)
+        hid[:, 0:T] = hidden.astype(BF16).astype(F32)
+        ht4[...] = jnp.zeros_like(ht4)
+        padded = hid[0:16, :]
+        turned = pltpu.roll(padded, 64, 1)
+        ht4[0:16, 0:256] = padded.astype(BF16)
+        ht4[16:32, 128:384] = turned.astype(BF16)
+        ht4[32:48, 384:640] = padded.astype(BF16)
+        ht4[48:64, 512:768] = turned.astype(BF16)
+
     @pl.when(parity == 0)
     def _():
         def first_step(kv, carry):
@@ -361,33 +368,25 @@
 
             @pl.when(kv == 0)
             def _():
-                kv_copy(second_half, 0, 0).start()
-
-            return carry
-
-        with jax.named_scope("even_first"):
-            lax.fori_loop(0, 2, first_step, 0)
-        with jax.named_scope("even_pass"):
-            kv_arrived(second_half, 1, 0)
-            kv_copy(second_half, 1, 0).start()
-            kv_arrived(second_half, 2, 0)
-            kv_copy(second_half, 2, 0).start()
-            kv_copy(second_half, 0, 1).start()
-            kv_arrived(second_half, 1, 1)
-            kv_copy(second_half, 1, 1).start()
+                kv_arrived(second_half, 2, 0)
+                kv_copy(second_half, 2, 0).start()
+                kv_copy(second_half, 0, 1).start()
+                kv_arrived(second_half, 1, 1)
+                kv_copy(second_half, 1, 1).start()
+
+            return carry
+
+        lax.fori_loop(0, 2, first_step, 0)
+        kv_arrived(second_half, 2, 1)
+        kv_copy(second_half, 2, 1).start()
+        hidden_layers()
 
         def second_step(kv, carry):
-            @pl.when(kv == 1)
-            def _():
-                kv_arrived(second_half, 2, 1)
-                kv_copy(second_half, 2, 1).start()
-                w_round_1()
-
             attend(second_half, kv, 3)
-            return carry
-
-        with jax.named_scope("even_second"):
-            lax.fori_loop(0, 2, second_step, 0)
+            pl.when(kv == 0)(w_round_1)
+            return carry
+
+        lax.fori_loop(0, 2, second_step, 0)
         w_round_2()
 
     @pl.when(parity == 1)
@@ -398,22 +397,18 @@
             attend(first_half, kv, 2)
             return carry
 
-        with jax.named_scope("odd_first"):
-            lax.fori_loop(0, 2, first_step, 0)
+        lax.fori_loop(0, 2, first_step, 0)
+        hidden_layers()
 
         def second_step(kv, carry):
             for slot in (1, 2, 3):
                 kv_arrived(second_half, slot, kv)
-
-            def between():
-                pl.when(kv == 0)(w_round_1)
-                pl.when(kv == 1)(w_round_2)
-
-            attend(second_half, kv, 4, between)
-            return carry
-
-        with jax.named_scope("odd_second"):
-            lax.fori_loop(0, 2, second_step, 0)
+            pl.when(kv == 0)(w_round_1)
+            pl.when(kv == 1)(w_round_2)
+            attend(second_half, kv, 4)
+            return carry
+
+        lax.fori_loop(0, 2, second_step, 0)
 
     with jax.named_scope("query_terms"):
         for copy in up_loads:
@@ -470,7 +465,7 @@
             fn(off)
             return carry
 
-        lax.fori_loop(1, 16, step, 0)
+        lax.fori_loop(1, 16, step, 0, unroll=True)
 
     with jax.named_scope("query_down"):
         down_terms(term_q, code_qt)
@@ -480,8 +475,6 @@
     with jax.named_scope("w_round_3"):
         w_arrived(7, 8, 9, 10)
         w_start(17, 18)
-        w_arrived(11, 12)
-        w_start(19)
 
     with jax.named_scope("value_gradient"):
         for half in range(2):
@@ -509,28 +502,31 @@
         each(lambda off: term_copy(1, off).start())
         rcv_v[0] = term_v[p]
 
-    with jax.named_scope("w_wait"):
+    with jax.named_scope("w_round_4"):
+        w_arrived(11, 12)
+        w_start(19)
+
+    def input_gradient():
         w_load.wait()
         w_arrived(4, *range(13, 20))
         code = (ADAPTER_SCALE * codes[...].astype(BF16).astype(F32)).T
         code = code[0:T, :].astype(BF16)
 
-    def dx_step(i, carry):
-        cols = pl.ds(pl.multiple_of(i * SHARD, SHARD), SHARD)
-        dx[:, cols] = (nt(gv[...], w[i]) + nn(code, dw[:, cols])).astype(BF16)
-        return carry
-
-    with jax.named_scope("dx_1"):
-        lax.fori_loop(0, 8, dx_step, 0, unroll=2)
+        def step(i, carry):
+            cols = pl.ds(pl.multiple_of(i * SHARD, SHARD), SHARD)
+            dx[:, cols] = (nt(gv[...], w[i]) + nn(code, dw[:, cols])).astype(BF16)
+            return carry
+
+        lax.fori_loop(0, DP, step, 0, unroll=2)
 
     with jax.named_scope("sum_dp"):
         each(lambda off: term_copy(0, off).wait_recv())
-        each(lambda off: term_copy(1, off).wait_recv())
+        sum_q = jnp.sum(rcv_q[...].astype(F32), axis=0)
         rs_src[...] = jnp.zeros_like(rs_src)
-        sum_q = jnp.sum(rcv_q[...].astype(F32), axis=0)
-        sum_v = jnp.sum(rcv_v[...].astype(F32), axis=0)
         for j in range(6):
             rs_src[:, j, :] = sum_q[:, j * D : (j + 1) * D]
+        each(lambda off: term_copy(1, off).wait_recv())
+        sum_v = jnp.sum(rcv_v[...].astype(F32), axis=0)
         for j in range(5):
             rs_src[:, 6 + j, :] = sum_v[:, j * D : (j + 1) * D]
 
@@ -540,7 +536,7 @@
             rs_src.at[target], rs_rcv.at[off], r_ssem.at[0, off], r_rsem.at[0, off], target, p
         )
 
-    def sum_copy(off, src=None):
+    def sum_copy(off):
         target = lax.rem(c + off, CTX)
         return remote(ag.at[c], ag.at[c], r_ssem.at[1, off], r_rsem.at[1, off], target, p)
 
@@ -548,21 +544,22 @@
         src = lax.rem(c + CTX - off, CTX)
         remote(ag.at[src], ag.at[src], r_ssem.at[1, off], r_rsem.at[1, off], src, p).wait_recv()
 
-    each(lambda off: row_copy(off).start())
+    for off in FAR_FIRST:
+        row_copy(off).start()
     rs_rcv[0] = rs_src[c]
 
-    with jax.named_scope("dx_2"):
-        lax.fori_loop(8, 12, dx_step, 0, unroll=2)
-
+    z = lax.rem(c, 8)
+    early = (z <= 2) | (z >= 6)
+    with jax.named_scope("dx_early"):
+        pl.when(early)(input_gradient)
     with jax.named_scope("sum_ctx"):
         each(lambda off: row_copy(off).wait_recv())
         gradient_scale = ADAPTER_SCALE / math.sqrt(DP * CTX * T)
         ag[c] = jnp.sum(rs_rcv[...], axis=0) * gradient_scale
-        each(lambda off: sum_copy(off).start())
-
-    with jax.named_scope("dx_3"):
-        lax.fori_loop(12, 16, dx_step, 0, unroll=2)
-
+        for off in FAR_FIRST:
+            sum_copy(off).start()
+    with jax.named_scope("dx_late"):
+        pl.when(jnp.logical_not(early))(input_gradient)
     with jax.named_scope("outputs"):
         each(sum_arrived)
         ag_out[...] = ag[...]

time: 72.6 us -> 67.7 us (0.933)
  Pallas kernels: 71.9 us -> 67 us
    pallas_call x1, Pallas kernels: 70.1 us -> 65.3 us  [on_device(): pl.pallas_call(kernel, out_shape=(pltpu.VMEM((CTX, 16, D), F32), pltpu.VM...]
where the time goes in v4:
time: 67.7 us; the launch traced here: 67.6 us
  Pallas kernels  67 us (99%)
    pallas_call x1, Pallas kernels, on_device(): pl.pallas_call(kernel, out_shape=(pltpu.VMEM((CTX, 16, D), F32), pltpu.VM...  65.3 us
    pallas_call x1, Pallas kernels, deliver(): pl.pallas_call(place, out_shape=(jax.ShapeDtypeStruct((16, SHARD), F32),...  1.72 us

profile of v4, /device:TPU:1, one launch (start us, length us, event | category | flops | bytes accessed | tf_op | source)
XLA Modules:
  0.0 67.6 jit_solution(9427723442116124456)
XLA Ops:
  0.6 65.3 %shard_map.137 = (f32[16,16,128]{2,1,0:T(8,128)S(1)}, bf16[192,8192]{1,0:T(8,128)(2,1)S(1)}) custom-call(bf16[192,8192]{1,0:T(8,128)(2,1)} %bitcast.5, bf16[192,4096]{1,0:T(8,128)(2,1)} %bitcast.6, bf16[192,512]{1,0:T(8,128)(2,1)} %bitcast.8, bf16[192,512]{1,0:T(8,128)(2,1)} %bitcast.9, bf16[192,4096]{1,0:T(8,128)(2,1)} %bitcast.7, bf16[512,512]{1,0:T(8,128)(2,1)} %w_hbm.1, ...), custom_call_target="tpu_custom_call" | custom-call | tf_op jit(solution)/shard_map/pallas_call | solution.py:663
  65.9 1.7 %shard_map.138 = (f32[16,512]{1,0:T(8,128)}, f32[16,256]{1,0:T(8,128)}, f32[16,512]{1,0:T(8,128)}, f32[16,32]{1,0:T(8,128)}, bf16[1,192,8192]{2,1,0:T(8,128)(2,1)}) custom-call(f32[16,16,128]{2,1,0:T(8,128)S(1)} %get-tuple-element.7.sums, bf16[192,8192]{1,0:T(8,128)(2,1)S(1)} %get-tuple-element.8.dx), custom_call_target="tpu_custom_call" | custom-call | tf_op jit(solution)/shard_map/pallas_call | solution.py:628

commit v5 on v4

--- a/solution.py
+++ b/solution.py
@@ -472,10 +472,6 @@
         each(lambda off: term_copy(0, off).start())
         rcv_q[0] = term_q[p]
 
-    with jax.named_scope("w_round_3"):
-        w_arrived(7, 8, 9, 10)
-        w_start(17, 18)
-
     with jax.named_scope("value_gradient"):
         for half in range(2):
             for d in range(1, 4):
@@ -502,10 +498,6 @@
         each(lambda off: term_copy(1, off).start())
         rcv_v[0] = term_v[p]
 
-    with jax.named_scope("w_round_4"):
-        w_arrived(11, 12)
-        w_start(19)
-
     def input_gradient():
         w_load.wait()
         w_arrived(4, *range(13, 20))
@@ -547,6 +539,14 @@
     for off in FAR_FIRST:
         row_copy(off).start()
     rs_rcv[0] = rs_src[c]
+
+    with jax.named_scope("w_round_3"):
+        w_arrived(7, 8, 9, 10)
+        w_start(17, 18)
+
+    with jax.named_scope("w_round_4"):
+        w_arrived(11, 12)
+        w_start(19)
 
     z = lax.rem(c, 8)
     early = (z <= 2) | (z >= 6)

time: 67.7 us -> 69.5 us (1.027)
  Pallas kernels: 67 us -> 68.8 us
    pallas_call x1, Pallas kernels: 65.3 us -> 67.1 us  [on_device(): pl.pallas_call(kernel, out_shape=(pltpu.VMEM((CTX, 16, D), F32), pltpu.VM...]
where the time goes in v5:
time: 69.5 us
  Pallas kernels  68.8 us (99%)
    pallas_call x1, Pallas kernels, on_device(): pl.pallas_call(kernel, out_shape=(pltpu.VMEM((CTX, 16, D), F32), pltpu.VM...  67.1 us
    pallas_call x1, Pallas kernels, deliver(): pl.pallas_call(place, out_shape=(jax.ShapeDtypeStruct((16, SHARD), F32),...  1.72 us

profile of v5, /device:TPU:1, one launch (start us, length us, event | category | flops | bytes accessed | tf_op | source)
XLA Modules:
  0.0 69.5 jit_solution(16216227598717800655)
XLA Ops:
  0.6 67.1 %shard_map.137 = (f32[16,16,128]{2,1,0:T(8,128)S(1)}, bf16[192,8192]{1,0:T(8,128)(2,1)S(1)}) custom-call(bf16[192,8192]{1,0:T(8,128)(2,1)} %bitcast.5, bf16[192,4096]{1,0:T(8,128)(2,1)} %bitcast.6, bf16[192,512]{1,0:T(8,128)(2,1)} %bitcast.8, bf16[192,512]{1,0:T(8,128)(2,1)} %bitcast.9, bf16[192,4096]{1,0:T(8,128)(2,1)} %bitcast.7, bf16[512,512]{1,0:T(8,128)(2,1)} %w_hbm.1, ...), custom_call_target="tpu_custom_call" | custom-call | tf_op jit(solution)/shard_map/pallas_call | solution.py:663
  67.7 1.7 %shard_map.138 = (f32[16,512]{1,0:T(8,128)}, f32[16,256]{1,0:T(8,128)}, f32[16,512]{1,0:T(8,128)}, f32[16,32]{1,0:T(8,128)}, bf16[1,192,8192]{2,1,0:T(8,128)(2,1)}) custom-call(f32[16,16,128]{2,1,0:T(8,128)S(1)} %get-tuple-element.7.sums, bf16[192,8192]{1,0:T(8,128)(2,1)S(1)} %get-tuple-element.8.dx), custom_call_target="tpu_custom_call" | custom-call | tf_op jit(solution)/shard_map/pallas_call | solution.py:628
